TPU v7x, 256 devices: a whole 4x4x8 slice. The times are simulated.
256 devices in a mesh: dp: 64 (over z, y, x_hi), pipe: 2 (over core), tensor: 2 (over x_lo).
Axes of the slice: x: 4 (x_hi: 2, x_lo: 2; x = x_hi * 2 + x_lo), y: 4, z: 8, core: 2. Of those that a mesh axis runs over, the one named last changes fastest.
Arguments:
- activations: bfloat16 [2, 32768, 4096], P('pipe', ('dp', 'tensor')), may hold values from -6 to 6
- norm_gain: float32 [2, 4096], P('pipe'), may hold values from 0.5 to 1.5
- value_weight: bfloat16 [2, 4096, 512], P('pipe', None, 'tensor'), may hold values from -0.75 to 0.75
- upstream_grad: bfloat16 [2, 32768, 512], P('pipe', 'dp', 'tensor'), may hold values from -4 to 4
- error_buffer: bfloat16 [2, 262144, 512], P('pipe', 'dp', 'tensor'), may hold values from -12 to 12
- prior_basis: float32 [2, 512, 32], P('pipe', 'tensor'), may hold values from -6 to 6
Outputs:
- received_grad: bfloat16 [2, 32768, 4096], P('pipe', ('dp', 'tensor'))
- left_factor: float32 [2, 8192, 32], P('pipe', 'tensor')
- right_factor: float32 [2, 512, 32], P('pipe', 'tensor')
- error_next: bfloat16 [2, 262144, 512], P('pipe', 'dp', 'tensor')
All inputs are finite; a program needn't handle non-finite values.
Results may differ from a plain program's by a relative error of at most 0.0049.
Values may be sent and summed in bfloat16 or wider, within the bound.
No kernel may reach another device: no remote copies, remote signals or barrier semaphores. Data moves between devices by JAX's collectives and lax.ppermute only.
A program may use at most 64 MiB of HBM per device.

v0:
```python
import math

import jax
import jax.numpy as jnp
from jax import lax
from jax.sharding import PartitionSpec as P

epsilon = 1e-05
clip_level = 0.25


def passed_along(value, axis, steps):
    count = lax.axis_size(axis)
    initial, last = (max(0, -steps), min(count, count - steps))
    return lax.ppermute(value, axis, [(source, source + steps) for source in range(initial, last)])


def orthonormal(factor, gram):
    lower = jnp.linalg.cholesky(gram)
    return lax.linalg.triangular_solve(lower, factor, left_side=False, lower=True, transpose_a=True)


def gram_of(factor):
    return jnp.dot(
        factor.T, factor, precision=lax.Precision.HIGHEST, preferred_element_type=jnp.float32
    )


def local(activations, norm_gain, value_weight, upstream_grad, error_buffer, prior_basis):
    activ = activations[0].astype(jnp.float32)
    gain_vector = norm_gain[0]
    weights = value_weight[0]
    upstream = upstream_grad[0]
    basis = prior_basis[0]
    inverse_rms = lax.rsqrt(jnp.mean(activ * activ, axis=-1, keepdims=True) + epsilon)
    normed = (activ * inverse_rms * gain_vector).astype(jnp.bfloat16)
    matching = upstream
    weight_grad = lax.dot_general(
        lax.all_gather(normed, "tensor", axis=0, tiled=True),
        matching,
        (((0,), (0,)), ((), ())),
        preferred_element_type=jnp.float32,
    )
    matching = upstream
    feature_grad = lax.psum_scatter(
        lax.dot_general(
            matching, weights, (((1,), (1,)), ((), ())), preferred_element_type=jnp.float32
        ),
        "tensor",
        scatter_dimension=0,
        tiled=True,
    )
    scaled = gain_vector * feature_grad
    along = jnp.mean(activ * scaled, axis=-1, keepdims=True)
    section_grad = (
        inverse_rms * scaled - activ * inverse_rms * inverse_rms * inverse_rms * along
    ).astype(jnp.bfloat16)
    received = passed_along(section_grad, "pipe", -1)
    merged = weight_grad + error_buffer[0].astype(jnp.float32)
    local_left = jnp.dot(
        merged, basis, precision=lax.Precision.HIGHEST, preferred_element_type=jnp.float32
    )
    summed = lax.psum(local_left, "dp")
    left = orthonormal(summed, gram_of(summed))
    local_right = lax.dot_general(
        merged,
        left,
        (((0,), (0,)), ((), ())),
        precision=lax.Precision.HIGHEST,
        preferred_element_type=jnp.float32,
    )
    replicas = lax.axis_size("dp")
    mean_right = lax.psum(local_right, "dp") / replicas
    approx = lax.dot_general(
        left,
        mean_right,
        (((1,), (1,)), ((), ())),
        precision=lax.Precision.HIGHEST,
        preferred_element_type=jnp.float32,
    )
    error_next = (merged - approx).astype(jnp.bfloat16)
    total = lax.psum(jnp.sum(mean_right * mean_right), ("pipe", "tensor"))
    entries = mean_right.size * lax.axis_size("pipe") * lax.axis_size("tensor")
    factor = jnp.minimum(1.0, clip_level * math.sqrt(entries) / jnp.sqrt(total + 1e-06))
    return (received[None], left[None], (mean_right * factor)[None], error_next[None])


def solution(mesh):
    placed = (
        P("pipe", ("dp", "tensor"), None),
        P("pipe", None),
        P("pipe", None, "tensor"),
        P("pipe", "dp", "tensor"),
        P("pipe", "dp", "tensor"),
        P("pipe", "tensor", None),
    )
    return jax.shard_map(
        local,
        mesh=mesh,
        in_specs=placed,
        out_specs=(
            P("pipe", ("dp", "tensor"), None),
            P("pipe", "tensor", None),
            P("pipe", "tensor", None),
            P("pipe", "dp", "tensor"),
        ),
        check_vma=False,
    )
```

profile of v0, /device:TPU:1, one launch (start us, length us, event | category | flops | bytes accessed | tf_op | source)
XLA Modules:
  0.0 1295.9 jit_solution(17232554093906886087)
XLA Ops:
  7.2 0.0 copy-start
  7.2 0.0 reduce-scatter.2.cloned.1.call-start
  7.2 1.5 copy-done
  8.8 5.5 fusion.11
  14.2 0.0 copy-start.6
  14.2 0.0 reduce-scatter.2.cloned.1.call-update
  14.2 0.0 all-gather.2.cloned.1.call-start
  14.3 108.2 %reduce-scatter.2.cloned.1.call-done = f32[256,4096]{1,0:T(8,128)} async-done(((f32[512,4096]{1,0:T(8,128)}), f32[256,4096]{1,0:T(8,128)}) %reduce-scatter.2.cloned.1.call-update) | async-done | bytes 4194320 | tf_op jit(solution)/shard_map/reduce_scatter | solution.py:45
  122.5 0.0 copy-start.2
  122.5 0.0 copy-start.3
  122.5 0.0 copy-done.6
  122.5 3.9 fusion.9
  126.4 0.1 copy-done.2
  126.6 0.7 copy-done.3
  127.2 0.0 copy-start.5
  127.2 3.9 fusion.8
  131.1 0.0 all-gather.2.cloned.1.call-update
  131.2 0.0 all-reduce.2.cloned.1.call-start
  131.2 0.0 copy-start.7
  131.2 3.9 collective-permute-start
  135.1 59.0 %all-gather.2.cloned.1.call-done = bf16[512,4096]{1,0:T(8,128)(2,1)} async-done(((bf16[256,4096]{1,0:T(8,128)(2,1)}), bf16[512,4096]{1,0:T(8,128)(2,1)}) %all-gather.2.cloned.1.call-update) | async-done | bytes 4194320 | tf_op jit(solution)/shard_map/all_gather | solution.py:39
  194.1 0.0 copy-done.5
  194.1 4.2 convolution_add_fusion
  198.3 0.0 copy-start.1
  198.3 1.9 copy-done.1
  200.2 0.0 copy-done.7
  200.2 4.7 fusion.15
  204.9 0.0 all-reduce.2.cloned.1.call-update
  205.0 0.0 collective-permute-done
  205.0 649.2 %all-reduce.2.cloned.1.call-done = f32[4096,32]{0,1:T(8,128)} async-done(((f32[4096,32]{0,1:T(8,128)}), f32[4096,32]{0,1:T(8,128)}) %all-reduce.2.cloned.1.call-update) | async-done | bytes 524304 | tf_op jit(solution)/shard_map/psum | solution.py:63
  854.2 1.8 fusion.24
  856.0 0.1 copy.10
  856.1 2.9 cholesky.16
  859.0 0.6 compare_reduce_fusion
  859.7 0.7 fusion.18
  860.3 2.4 custom-call.6
  862.8 1.7 fusion.19
  864.5 0.0 copy-start.4
  864.5 4.6 fusion.25
  869.1 300.8 %psum.22 = f32[256,32]{0,1:T(8,128)S(1)} all-reduce(f32[256,32]{0,1:T(8,128)S(1)} %fusion.25), channel_id=1, replica_groups=mesh['dp'=64,'pipe'=2,'tensor'=2] {'dp'}, use_global_device_ids=true, to_apply=%region_6.7 | all-reduce | flops 8192 | bytes 65536 | tf_op jit(solution)/shard_map/psum | solution.py:73
  1169.9 0.6 multiply_reduce_fusion
  1170.5 6.3 fusion.3
  1176.8 0.0 copy-done.4
  1176.8 108.2 %psum.23 = f32[]{:T(128)} all-reduce(f32[]{:T(128)} %multiply_reduce_fusion), channel_id=1, replica_groups=mesh['dp'=64,'pipe'=2,'tensor'=2] {'pipe','tensor'}, use_global_device_ids=true, to_apply=%region_8.9 | all-reduce | flops 1 | bytes 8 | tf_op jit(solution)/shard_map/psum | solution.py:82
  1285.7 0.6 multiply_bitcast_fusion
  1286.3 3.1 copy.13
  (3 shorter events, 0.0 us)
Async XLA Ops:
  7.2 1.6 copy-start
  7.2 115.3 %reduce-scatter.2.cloned.1.call-start = ((), (), s32[]{:S(2)}) async-start(), calls=%async_computation.1 | async-start | bytes 12582912 | tf_op jit(solution)/shard_map/reduce_scatter | solution.py:45
  14.2 108.3 %copy-start.6 = (f32[1,4096]{1,0:T(1,128)S(1)}, f32[1,4096]{1,0:T(1,128)}, u32[]{:S(2)}) copy-start(f32[1,4096]{1,0:T(1,128)} %param.7) | copy-start | bytes 49156
  14.2 179.9 %all-gather.2.cloned.1.call-start = ((), (), s32[]{:S(2)}) async-start(), calls=%async_computation.2 | async-start | bytes 6291456 | tf_op jit(solution)/shard_map/all_gather | solution.py:39
  122.5 4.0 copy-start.2
  122.5 4.7 copy-start.3
  127.2 66.9 %copy-start.5 = (bf16[1,512,256]{2,1,0:T(8,128)(2,1)S(1)}, bf16[1,512,256]{2,1,0:T(8,128)(2,1)}, u32[]{:S(2)}) copy-start(bf16[1,512,256]{2,1,0:T(8,128)(2,1)} %param.9) | copy-start | bytes 786436
  131.2 723.1 %all-reduce.2.cloned.1.call-start = ((), (), s32[]{:S(2)}) async-start(), calls=%async_computation.3 | async-start | bytes 1048576 | tf_op jit(solution)/shard_map/psum | solution.py:63
  131.2 69.0 %copy-start.7 = (f32[1,256,32]{1,2,0:T(8,128)S(1)}, f32[1,256,32]{1,2,0:T(8,128)}, u32[]{:S(2)}) copy-start(f32[1,256,32]{1,2,0:T(8,128)} %param.11) | copy-start | bytes 98308
  131.2 73.8 %collective-permute-start = (bf16[256,4096]{1,0:T(8,128)(2,1)}, bf16[256,4096]{1,0:T(8,128)(2,1)}, u32[]{:S(2)}, u32[]{:S(2)}) collective-permute-start(bf16[256,4096]{1,0:T(8,128)(2,1)} %get-tuple-element.7), channel_id=1, source_target_pairs={{2,0},{3,1},{6,4},{7,5},{10,8},{11,9},{14,12},{15,13},{18,16},{19,... | collective-permute-start | bytes 6291464 | tf_op jit(solution)/shard_map/ppermute | solution.py:15
  198.3 1.9 copy-start.1
  864.5 312.3 %copy-start.4 = (f32[4096,32]{0,1:T(8,128)}, f32[4096,32]{0,1:T(8,128)S(1)}, u32[]{:S(2)}) copy-start(f32[4096,32]{0,1:T(8,128)S(1)} %fusion.19) | copy-start | bytes 1572868
Sparse Core Ops, SparseCore 0:
  14.4 108.1 reduce-scatter.1
  131.3 62.8 all-gather.1
  205.1 649.0 all-reduce.1
where the time goes:
time: 1300 us
  waiting for transfers between devices  817 us (63%)
  blocking collectives  409 us (31%)
  matrix products  28.7 us (2%)
  other arithmetic  15.7 us (1%)
  between operations  14.5 us (1%)
    psum x1, waiting for transfers between devices, local(): summed = lax.psum(local_left, 'dp')  649 us
    psum x1, blocking collectives, local(): mean_right = lax.psum(local_right, 'dp') / replicas  301 us
    reduce_scatter x1, waiting for transfers between devices, local(): lax.psum_scatter(lax.dot_general(matching, weights, (((1,), (1,)), ((), (...  108 us
    psum x1, blocking collectives, local(): total = lax.psum(jnp.sum(mean_right * mean_right), ('pipe', 'tensor'))  108 us
    all_gather x1, waiting for transfers between devices, local(): lax.all_gather(normed, 'tensor', axis=0, tiled=True)  59 us
  transfers between devices with their start and end apart: 4, of which 3 were waited for; matrix products, arithmetic and copies ran while one was open for 1% of the time, Pallas kernels for 0%

commit v1 on v0

v1 whole, which is shorter than its diff:
```python
import math

import jax
import jax.numpy as jnp
from jax import lax
from jax.sharding import Mesh, PartitionSpec as P

epsilon = 1e-05
clip_level = 0.25
DP = ("z", "y", "xh")
f32 = jnp.float32
bf16 = jnp.bfloat16


def halves(value):
    high = lax.reduce_precision(value, exponent_bits=8, mantissa_bits=7)
    return high.astype(bf16), (value - high).astype(bf16)


def dot(left, right, left_dim, right_dim):
    return lax.dot_general(
        left, right, (((left_dim,), (right_dim,)), ((), ())), preferred_element_type=f32
    )


def exchange(chunks, axis):
    return lax.all_to_all(chunks, axis, 0, 0, tiled=False)


def spread(value, axis, count):
    return exchange(jnp.broadcast_to(value[None], (count,) + value.shape), axis)


def exact(left, right, left_dim, right_dim):
    return lax.dot_general(
        left,
        right,
        (((left_dim,), (right_dim,)), ((), ())),
        precision=lax.Precision.HIGHEST,
        preferred_element_type=f32,
    )


def local(activations, norm_gain, value_weight, upstream_grad, error_buffer, prior_basis):
    activ_own = activations[0]
    gain = norm_gain[0]
    weights = value_weight[0]
    upstream = upstream_grad[0]
    error = error_buffer[0]
    basis = prior_basis[0]
    tokens, width = activ_own.shape
    columns = upstream.shape[1]
    rank = basis.shape[1]
    shard = lax.axis_index("tensor")
    swap = [(0, 1), (1, 0)]

    up_own = lax.dynamic_slice_in_dim(upstream, shard * tokens, tokens, 0)
    up_give = lax.dynamic_slice_in_dim(upstream, (1 - shard) * tokens, tokens, 0)
    up_other = lax.ppermute(up_give, "tensor", swap)
    basis_other = lax.ppermute(basis, "tensor", swap)

    beside = [(2, 7), (7, 2), (3, 6), (6, 3)]
    weights_other = lax.ppermute(weights, ("xh", "pipe", "tensor"), beside)
    up_other, basis_other, activ_late = lax.optimization_barrier((up_other, basis_other, activ_own))
    activ_other = lax.ppermute(activ_late, "tensor", swap)

    def normalised(rows):
        wide = rows.astype(f32)
        inverse = lax.rsqrt(jnp.mean(wide * wide, axis=-1, keepdims=True) + epsilon)
        return wide, inverse, (wide * inverse * gain).astype(bf16)

    activ, inverse_rms, normed_own = normalised(activ_own)

    basis_parts = jnp.concatenate(halves(basis), axis=1)
    from_error = dot(basis_parts, error, 0, 1)
    from_error = from_error[:rank] + from_error[rank:]
    own_v = exact(basis, up_own.astype(f32), 0, 1)
    other_v = exact(basis_other, up_other.astype(f32), 0, 1)
    both_v = jnp.concatenate([own_v, other_v], axis=0)
    product = dot(jnp.concatenate(halves(both_v), axis=0), normed_own, 1, 0)
    product = product[: 2 * rank] + product[2 * rank :]
    own_p = product[:rank] + from_error
    other_p = product[rank:]
    first = jnp.where(shard == 0, own_p, other_p)
    second = jnp.where(shard == 0, other_p, own_p)
    terms = jnp.concatenate([first, second], axis=0)

    n_y, n_z, n_x = lax.axis_size("y"), lax.axis_size("z"), lax.axis_size("xh")
    n_t = lax.axis_size("tensor")
    part_y = width // n_y
    part_z = part_y // n_z
    terms = terms.reshape(n_t * rank, n_y, part_y).transpose(1, 0, 2)
    terms = exchange(terms, "y").sum(0)
    terms = terms.reshape(n_t * rank, n_z, part_z).transpose(1, 0, 2)
    terms = exchange(terms, "z").sum(0).reshape(1, n_t, rank, part_z)
    terms = jnp.broadcast_to(terms, (n_x, n_t, rank, part_z)).reshape(n_x * n_t, rank, part_z)
    summed = exchange(terms, ("xh", "tensor")).sum(0)
    summed = spread(summed, "z", n_z).transpose(1, 0, 2).reshape(rank, part_y)
    summed = spread(summed, "y", n_y).transpose(1, 0, 2).reshape(rank, width)

    _, _, normed_other = normalised(activ_other)
    low = jnp.where(shard == 0, normed_own, normed_other)
    high = jnp.where(shard == 0, normed_other, normed_own)
    normed = jnp.concatenate([low, high], axis=0)
    merged = dot(normed, upstream, 0, 0) + error.astype(f32)

    summed_parts = jnp.concatenate(halves(summed), axis=0)
    from_tokens = dot(summed_parts, normed, 1, 1)
    from_tokens = from_tokens[:rank] + from_tokens[rank:]
    direct = dot(summed_parts, error, 1, 0)
    local_right = direct[:rank] + direct[rank:]
    through = dot(jnp.concatenate(halves(from_tokens), axis=0), upstream, 1, 0)
    local_right = local_right + through[:rank] + through[rank:]

    right_terms = spread(local_right, ("y", "xh"), n_y * n_x).sum(0)
    right_sum = spread(right_terms, "z", n_z).sum(0)

    gram = exact(summed, summed, 1, 1)
    lower = jnp.linalg.cholesky(gram)
    left = lax.linalg.triangular_solve(lower, summed, left_side=True, lower=True)
    mean_right = lax.linalg.triangular_solve(lower, right_sum, left_side=True, lower=True)
    mean_right = mean_right / (n_y * n_z * n_x)

    left_high, left_low = halves(left)
    right_high, right_low = halves(mean_right)
    approx = dot(
        jnp.concatenate([left_high, left_low, left_high], axis=0),
        jnp.concatenate([right_high, right_high, right_low], axis=0),
        0,
        0,
    )
    error_next = (merged - approx).astype(bf16)

    squares = jnp.sum(mean_right * mean_right)[None, None]
    squares = squares + lax.ppermute(squares, "pipe", swap)
    total = (squares + lax.ppermute(squares, "tensor", swap))[0, 0]
    entries = mean_right.size * lax.axis_size("pipe") * n_t
    factor = jnp.minimum(1.0, clip_level * math.sqrt(entries) / jnp.sqrt(total + 1e-06))

    feature_grad = dot(up_own, weights, 1, 1) + dot(up_other, weights_other, 1, 1)
    scaled = gain * feature_grad
    along = jnp.mean(activ * scaled, axis=-1, keepdims=True)
    section_grad = (
        inverse_rms * scaled - activ * inverse_rms * inverse_rms * inverse_rms * along
    ).astype(bf16)
    received = lax.ppermute(section_grad, "pipe", [(1, 0)])
    return (
        received[None],
        left.T[None],
        (mean_right * factor).T[None],
        error_next[None],
    )


def solution(mesh):
    sizes = (8, 4, 2) if mesh.shape["dp"] == 64 else (mesh.shape["dp"], 1, 1)
    inner = Mesh(
        mesh.devices.reshape(sizes + (mesh.shape["pipe"], mesh.shape["tensor"])),
        DP + ("pipe", "tensor"),
    )
    return jax.shard_map(
        local,
        mesh=inner,
        in_specs=(
            P("pipe", DP + ("tensor",), None),
            P("pipe", None),
            P("pipe", None, "tensor"),
            P("pipe", DP, "tensor"),
            P("pipe", DP, "tensor"),
            P("pipe", "tensor", None),
        ),
        out_specs=(
            P("pipe", DP + ("tensor",), None),
            P("pipe", "tensor", None),
            P("pipe", "tensor", None),
            P("pipe", DP, "tensor"),
        ),
        check_vma=False,
    )
```

time: 1300 us -> 156 us (0.12)
  waiting for transfers between devices: 817 us -> 41.2 us
  blocking collectives: 409 us -> 0 us
  starting transfers between devices: 4.03 us -> 46.1 us
    psum x1 -> x0, waiting for transfers between devices: 649 us -> none  [local(): summed = lax.psum(local_left, 'dp')]
    psum x2 -> x0, blocking collectives: 409 us -> none  [the longest x1 301 us: local(): mean_right = lax.psum(local_right, 'dp') / replicas]
    reduce_scatter x1 -> x0, waiting for transfers between devices: 108 us -> none  [local(): lax.psum_scatter(lax.dot_general(matching, weights, (((1,), (1,)), ((), (...]
    all_gather x1 -> x0, waiting for transfers between devices: 59 us -> none  [local(): lax.all_gather(normed, 'tensor', axis=0, tiled=True)]
    all_to_all x0 -> x7, starting transfers between devices: none -> 34.9 us  [exchange(): return lax.all_to_all(chunks, axis, 0, 0, tiled=False)]
    all_to_all x0 -> x7, waiting for transfers between devices: none -> 26.4 us  [exchange(): return lax.all_to_all(chunks, axis, 0, 0, tiled=False)]
    ppermute x1 -> x7, waiting for transfers between devices: 0.01 us -> 14.8 us  [the longest x1 12.5 us: local(): weights_other = lax.ppermute(weights, ('xh', 'pipe', 'tensor'), beside)]
    dot_general x6 -> x12, matrix products: 27 us -> 29.4 us  [the longest x9 27 us: dot(): lax.dot_general(left, right, (((left_dim,), (right_dim,)), ((), ())), pre...]
  transfers between devices with their start and end apart: 4 -> 14, of which waited for: 3 -> 9; matrix products, arithmetic and copies ran while one was open for 1% -> 36% of each run, Pallas kernels for 0% -> 0%
where the time goes in v1:
time: 156 us; the launch traced here: 155 us
  starting transfers between devices  46.1 us (30%)
  waiting for transfers between devices  41.2 us (26%)
  matrix products  31.7 us (20%)
  other arithmetic  22.3 us (14%)
  local copies, waits for them, and re-layouts  10.4 us (7%)
  between operations  2.85 us (2%)
    all_to_all x7, starting transfers between devices, exchange(): return lax.all_to_all(chunks, axis, 0, 0, tiled=False)  34.9 us
    dot_general x9, matrix products, dot(): lax.dot_general(left, right, (((left_dim,), (right_dim,)), ((), ())), pre...  27 us
    all_to_all x7, waiting for transfers between devices, exchange(): return lax.all_to_all(chunks, axis, 0, 0, tiled=False)  26.4 us
    ppermute x1, waiting for transfers between devices, local(): weights_other = lax.ppermute(weights, ('xh', 'pipe', 'tensor'), beside)  12.5 us
    ppermute x1, starting transfers between devices, local(): weights_other = lax.ppermute(weights, ('xh', 'pipe', 'tensor'), beside)  5.35 us
    select_n x1, other arithmetic, local(): low = jnp.where(shard == 0, normed_own, normed_other)  5.18 us
    convert_element_type x1, other arithmetic, local(): section_grad = (inverse_rms * scaled - activ * inverse_rms * inverse_rms...  4.86 us
    unnamed x18, local copies, waits for them, and re-layouts  4.17 us
  transfers between devices with their start and end apart: 14, of which 9 were waited for; matrix products, arithmetic and copies ran while one was open for 36% of the time, Pallas kernels for 0%

profile of v1, /device:TPU:1, one launch (start us, length us, event | category | flops | bytes accessed | tf_op | source)
XLA Modules:
  0.0 154.5 jit_solution(1196422606929065053)
XLA Ops:
  0.6 5.4 %collective-permute-start.2 = (bf16[4096,256]{1,0:T(8,128)(2,1)}, bf16[4096,256]{1,0:T(8,128)(2,1)}, u32[]{:S(2)}, u32[]{:S(2)}) collective-permute-start(bf16[4096,256]{1,0:T(8,128)(2,1)} %bitcast.104), channel_id=1, source_target_pairs={{2,7},{7,2},{3,6},{6,3},{10,15},{15,10},{11,14},{14,11},{18,23},{2... | collective-permute-start | bytes 6291464 | tf_op jit(solution)/shard_map/ppermute | solution.py:63
  6.1 0.7 dynamic-slice_bitcast_fusion
  6.8 1.4 collective-permute-start
  8.2 0.9 reduce-precision_convert_fusion.5
  9.2 2.5 %fusion.18 = f32[64,4096]{1,0:T(8,128)S(1)} fusion(bf16[1,4096,256]{2,1,0:T(8,128)(2,1)} %param.10, bf16[256,32]{0,1:T(8,128)(2,1)S(1)} %get-tuple-element.28, bf16[256,32]{0,1:T(8,128)(2,1)S(1)} %get-tuple-element.27), kind=kOutput, calls=%fused_computation.27 | convolution fusion | flops 134283264 | bytes 3178496 | tf_op jit(solution)/shard_map/dot_general | solution.py:21
  11.7 2.7 %fusion.33 = f32[256,4096]{1,0:T(8,128)} fusion(bf16[1,512,256]{2,1,0:T(8,128)(2,1)S(1)} %copy-done, s32[]{:T(128)S(6)} %select_n.34, bf16[1,4096,256]{2,1,0:T(8,128)(2,1)S(1)} %copy-done.3), kind=kOutput, calls=%fused_computation.58 | convolution fusion | flops 536870912 | bytes 6422532 | tf_op jit(solution)/shard_map/dot_general | solution.py:21
  14.4 0.9 convolution_bitcast_fusion
  15.4 1.0 fusion.74
  16.4 0.8 reduce-precision_convert_fusion.3
  17.2 12.5 %collective-permute-done.2 = bf16[4096,256]{1,0:T(8,128)(2,1)} collective-permute-done((bf16[4096,256]{1,0:T(8,128)(2,1)}, bf16[4096,256]{1,0:T(8,128)(2,1)}, u32[]{:S(2)}, u32[]{:S(2)}) %collective-permute-start.2) | collective-permute-done | bytes 2097184 | tf_op jit(solution)/shard_map/ppermute | solution.py:63
  29.7 6.6 %fusion.13 = (f32[256]{0:T(256)S(1)}, f32[256]{0:T(256)}, f32[256,4096]{1,0:T(8,128)}) fusion(bf16[1,256,4096]{2,1,0:T(8,128)(2,1)S(1)} %copy-done.1, f32[256,4096]{1,0:T(8,128)} %fusion.33, bf16[256,256]{1,0:T(8,128)(2,1)S(1)} %collective-permute-done, bf16[4096,256]{1,0:T(8,128)(2,1)} %collective-permute-done.2, f32[4096]{0:T(1024)S(1)} %bitcast.108), kind=kOutput, calls=%fused_computation.21 | convolution fusion | flops 544210432 | bytes 12732416 | tf_op jit(solution)/shard_map/dot_general | solution.py:21
  36.3 0.8 fusion.39
  37.5 1.0 copy.32
  38.5 4.4 %all-to-all-start = ((f32[4,64,1024]{2,1,0:T(8,128)}), f32[4,64,1024]{2,1,0:T(8,128)S(1)}, u32[]{:S(2)}, u32[]{:S(2)}) async-start(f32[4,64,1024]{2,1,0:T(8,128)} %bitcast.102), calls=%async_computation | async-start | bytes 2097152 | tf_op jit(solution)/shard_map/all_to_all | solution.py:27
  42.9 9.7 %all-to-all-done = f32[4,64,1024]{2,1,0:T(8,128)S(1)} async-done(((f32[4,64,1024]{2,1,0:T(8,128)}), f32[4,64,1024]{2,1,0:T(8,128)S(1)}, u32[]{:S(2)}, u32[]{:S(2)}) %all-to-all-start) | async-done | bytes 1048608 | tf_op jit(solution)/shard_map/all_to_all | solution.py:27
  52.6 0.8 reduce_sum.83
  53.4 1.0 copy.29
  54.4 0.8 copy.22
  55.2 8.2 %all-to-all-start.1 = ((f32[8,64,128]{2,1,0:T(8,128)}), f32[8,64,128]{2,1,0:T(8,128)S(1)}, u32[]{:S(2)}, u32[]{:S(2)}) async-start(f32[8,64,128]{2,1,0:T(8,128)} %copy.22), calls=%async_computation.1 | async-start | bytes 524288 | tf_op jit(solution)/shard_map/all_to_all | solution.py:27
  63.4 4.9 %fusion.8 = bf16[256,4096]{1,0:T(8,128)(2,1)} fusion(f32[256,4096]{1,0:T(8,128)} %get-tuple-element.29, f32[256]{0:T(256)S(1)} %broadcast_multiply_fusion, f32[256]{0:T(256)S(1)} %add_rsqrt_fusion.1, bf16[1,256,4096]{2,1,0:T(8,128)(2,1)S(1)} %copy-done.1), kind=kLoop, calls=%fused_computation.16 | loop fusion | flops 8388608 | bytes 8390656 | tf_op jit(solution)/shard_map/convert_element_type | solution.py:145
  68.2 2.6 %collective-permute-start.3 = (bf16[256,4096]{1,0:T(8,128)(2,1)}, bf16[256,4096]{1,0:T(8,128)(2,1)}, u32[]{:S(2)}, u32[]{:S(2)}) collective-permute-start(bf16[256,4096]{1,0:T(8,128)(2,1)} %fusion.8), channel_id=1, source_target_pairs={{2,0},{3,1},{6,4},{7,5},{10,8},{11,9},{14,12},{15,13},{18,16},{19,... | collective-permute-start | bytes 6291464 | tf_op jit(solution)/shard_map/ppermute | solution.py:146
  70.9 2.1 %fusion.10 = f32[256]{0:T(256)S(1)} fusion(bf16[256,4096]{1,0:T(8,128)(2,1)} %collective-permute-done.4), kind=kLoop, calls=%fused_computation.18 | loop fusion | flops 3145472 | bytes 2098176 | tf_op jit(solution)/shard_map/reduce_sum | solution.py:69
  73.6 4.0 %all-to-all-start.2 = ((f32[4,32,128]{2,1,0:T(8,128)}), f32[4,32,128]{2,1,0:T(8,128)S(1)}, u32[]{:S(2)}, u32[]{:S(2)}) async-start(f32[4,32,128]{2,1,0:T(8,128)} %bitcast.12), calls=%async_computation.2 | async-start | bytes 131072 | tf_op jit(solution)/shard_map/all_to_all | solution.py:27
  77.7 4.5 %all-to-all-done.2 = f32[4,32,128]{2,1,0:T(8,128)S(1)} async-done(((f32[4,32,128]{2,1,0:T(8,128)}), f32[4,32,128]{2,1,0:T(8,128)S(1)}, u32[]{:S(2)}, u32[]{:S(2)}) %all-to-all-start.2) | async-done | bytes 65568 | tf_op jit(solution)/shard_map/all_to_all | solution.py:27
  82.1 0.7 broadcast_in_dim.55
  82.8 6.6 %all-to-all-start.3 = ((f32[8,32,128]{2,1,0:T(8,128)}), f32[8,32,128]{2,1,0:T(8,128)S(1)}, u32[]{:S(2)}, u32[]{:S(2)}) async-start(f32[8,32,128]{2,1,0:T(8,128)} %broadcast_in_dim.55), calls=%async_computation.3 | async-start | bytes 262144 | tf_op jit(solution)/shard_map/all_to_all | solution.py:27
  89.4 5.2 %broadcast_select_fusion.1 = (bf16[256,4096]{1,0:T(8,128)(2,1)}, bf16[256,4096]{1,0:T(8,128)(2,1)}) fusion(pred[]{:T(512)S(6)} %eq.2, f32[4096]{0:T(1024)S(1)} %bitcast.110, f32[256]{0:T(256)S(1)} %add_rsqrt_fusion, bf16[256,4096]{1,0:T(8,128)(2,1)} %collective-permute-done.4, f32[256]{0:T(256)S(1)} %add_rsqrt_fusion.1, bf16[1,256,4096]{2,1,0:T(8,128)(2,1)S(1)} %copy-done.1), kind=kLoop, calls=%fused_computation.30 | loop fusion | flops 10485760 | bytes 8407041 | tf_op jit(solution)/shard_map/jit(_where)/select_n | solution.py:102
  94.6 2.7 %all-to-all-done.3 = f32[8,32,128]{2,1,0:T(8,128)S(1)} async-done(((f32[8,32,128]{2,1,0:T(8,128)}), f32[8,32,128]{2,1,0:T(8,128)S(1)}, u32[]{:S(2)}, u32[]{:S(2)}) %all-to-all-start.3) | async-done | bytes 131104 | tf_op jit(solution)/shard_map/all_to_all | solution.py:27
  97.4 0.8 broadcast_in_dim.57
  98.2 3.7 %all-to-all-start.4 = ((f32[4,32,1024]{2,1,0:T(8,128)}), f32[4,32,1024]{2,1,0:T(8,128)S(1)}, u32[]{:S(2)}, u32[]{:S(2)}) async-start(f32[4,32,1024]{2,1,0:T(8,128)} %broadcast_in_dim.57), calls=%async_computation.4 | async-start | bytes 1048576 | tf_op jit(solution)/shard_map/all_to_all | solution.py:27
  101.9 6.3 %convolution_add_fusion = f32[4096,256]{1,0:T(8,128)} fusion(bf16[256,4096]{1,0:T(8,128)(2,1)} %get-tuple-element.13, bf16[256,4096]{1,0:T(8,128)(2,1)} %get-tuple-element.12, bf16[1,4096,256]{2,1,0:T(8,128)(2,1)} %param.10, bf16[1,512,256]{2,1,0:T(8,128)(2,1)S(1)} %copy-done), kind=kOutput, calls=%fused_computation.4 | convolution fusion | flops 1084227584 | bytes 10747904 | tf_op jit(solution)/shard_map/dot_general | solution.py:21
  109.4 3.1 %fusion.15 = f32[64,512]{1,0:T(8,128)S(1)} fusion(bf16[256,4096]{1,0:T(8,128)(2,1)} %get-tuple-element.13, bf16[256,4096]{1,0:T(8,128)(2,1)S(1)} %copy-done.4, bf16[32,4096]{1,0:T(8,128)(2,1)S(1)} %get-tuple-element.19, bf16[32,4096]{1,0:T(8,128)(2,1)S(1)} %get-tuple-element.18), kind=kOutput, calls=%fused_computation.24 | convolution fusion | flops 277872640 | bytes 4849664 | tf_op jit(solution)/shard_map/dot_general | solution.py:21
  113.2 0.7 broadcast_in_dim.59
  113.9 4.1 %all-to-all-start.5 = ((f32[8,32,256]{2,1,0:T(8,128)}), f32[8,32,256]{2,1,0:T(8,128)S(1)}, u32[]{:S(2)}, u32[]{:S(2)}) async-start(f32[8,32,256]{2,1,0:T(8,128)} %broadcast_in_dim.59), calls=%async_computation.5 | async-start | bytes 524288 | tf_op jit(solution)/shard_map/all_to_all | solution.py:27
  118.0 2.9 %cholesky.16 = f32[32,32]{1,0:T(8,128)S(1)} custom-call(f32[32,32]{1,0:T(8,128)S(1)} %fusion.61), custom_call_target="Cholesky" | custom-call | tf_op jit(solution)/shard_map/jit(cholesky)/cholesky | solution.py:119
  121.6 4.0 %all-to-all-done.5 = f32[8,32,256]{2,1,0:T(8,128)S(1)} async-done(((f32[8,32,256]{2,1,0:T(8,128)}), f32[8,32,256]{2,1,0:T(8,128)S(1)}, u32[]{:S(2)}, u32[]{:S(2)}) %all-to-all-start.5) | async-done | bytes 262176 | tf_op jit(solution)/shard_map/all_to_all | solution.py:27
  125.7 0.7 broadcast_in_dim.60
  126.4 3.9 %all-to-all-start.6 = ((f32[8,32,256]{2,1,0:T(8,128)}), f32[8,32,256]{2,1,0:T(8,128)S(1)}, u32[]{:S(2)}, u32[]{:S(2)}) async-start(f32[8,32,256]{2,1,0:T(8,128)} %broadcast_in_dim.60), calls=%async_computation.6 | async-start | bytes 524288 | tf_op jit(solution)/shard_map/all_to_all | solution.py:27
  130.3 0.7 fusion.56
  131.0 2.4 %custom-call.8 = f32[1,32,32]{1,2,0:T(8,128)S(1)} custom-call(f32[1,32,32]{2,1,0:T(8,128)S(1)} %fusion.56), custom_call_target="InvertDiagBlocksLowerTriangular" | custom-call | tf_op jit(solution)/shard_map/triangular_solve | solution.py:120
  133.4 1.5 fusion.26
  134.9 5.0 %all-to-all-done.6 = f32[8,32,256]{2,1,0:T(8,128)S(1)} async-done(((f32[8,32,256]{2,1,0:T(8,128)}), f32[8,32,256]{2,1,0:T(8,128)S(1)}, u32[]{:S(2)}, u32[]{:S(2)}) %all-to-all-start.6) | async-done | bytes 262176 | tf_op jit(solution)/shard_map/all_to_all | solution.py:27
  139.9 0.8 multiply_reduce_fusion
  140.8 1.4 collective-permute-done.5
  143.4 1.6 %collective-permute-start.6 = (f32[1,1]{1,0:T(1,128)}, f32[1,1]{1,0:T(1,128)}, u32[]{:S(2)}, u32[]{:S(2)}) collective-permute-start(f32[1,1]{1,0:T(1,128)} %add.85), channel_id=1, source_target_pairs={{0,1},{1,0},{2,3},{3,2},{4,5},{5,4},{6,7},{7,6},{8,9},{9,8},{10,11... | collective-permute-start | bytes 20 | tf_op jit(solution)/shard_map/ppermute | solution.py:136
  145.0 0.9 collective-permute-done.6
  147.2 4.3 %fusion.4 = bf16[1,4096,256]{2,1,0:T(8,128)(2,1)} fusion(f32[4096,256]{1,0:T(8,128)} %convolution_add_fusion, bf16[32,4096]{1,0:T(8,128)(2,1)S(1)} %get-tuple-element.17, bf16[32,4096]{1,0:T(8,128)(2,1)S(1)} %get-tuple-element.16, bf16[32,256]{1,0:T(8,128)(2,1)S(1)} %get-tuple-element.25, bf16[32,256]{1,0:T(8,128)(2,1)S(1)} %get-tuple-element.24), kind=kOutput, calls=%fused_computation.12 | convolution fusion | flops 205930496 | bytes 6848512 | tf_op jit(solution)/shard_map/dot_general | solution.py:21
  151.4 3.1 %copy.34 = bf16[1,256,4096]{2,1,0:T(8,128)(2,1)} copy(bf16[1,256,4096]{2,1,0:T(8,128)(2,1)} %bitcast.6) | data formatting | bytes 4194304
  (49 shorter events, 4.4 us)
Async XLA Ops:
  0.6 5.5 %copy-start = (bf16[1,512,256]{2,1,0:T(8,128)(2,1)S(1)}, bf16[1,512,256]{2,1,0:T(8,128)(2,1)}, u32[]{:S(2)}) copy-start(bf16[1,512,256]{2,1,0:T(8,128)(2,1)} %param.9) | copy-start | bytes 786436
  0.6 29.1 %collective-permute-start.2 = (bf16[4096,256]{1,0:T(8,128)(2,1)}, bf16[4096,256]{1,0:T(8,128)(2,1)}, u32[]{:S(2)}, u32[]{:S(2)}) collective-permute-start(bf16[4096,256]{1,0:T(8,128)(2,1)} %bitcast.104), channel_id=1, source_target_pairs={{2,7},{7,2},{3,6},{6,3},{10,15},{15,10},{11,14},{14,11},{18,23},{2... | collective-permute-start | bytes 6291464 | tf_op jit(solution)/shard_map/ppermute | solution.py:63
  6.0 9.3 %collective-permute-start.1 = (f32[256,32]{0,1:T(8,128)}, f32[256,32]{0,1:T(8,128)}, u32[]{:S(2)}, u32[]{:S(2)}) collective-permute-start(f32[256,32]{0,1:T(8,128)} %bitcast.112), channel_id=1, source_target_pairs={{0,1},{1,0},{2,3},{3,2},{4,5},{5,4},{6,7},{7,6},{8,9},{9,8},{10,11... | collective-permute-start | bytes 98312 | tf_op jit(solution)/shard_map/ppermute | solution.py:60
  6.8 8.5 %collective-permute-start = (bf16[256,256]{1,0:T(8,128)(2,1)}, bf16[256,256]{1,0:T(8,128)(2,1)S(1)}, u32[]{:S(2)}, u32[]{:S(2)}) collective-permute-start(bf16[256,256]{1,0:T(8,128)(2,1)} %dynamic-slice_bitcast_fusion), channel_id=1, source_target_pairs={{0,1},{1,0},{2,3},{3,2},{4,5},{5,4},{6,7},{7,6},{8,9},{9,8},{10,11... | collective-permute-start | bytes 393224 | tf_op jit(solution)/shard_map/ppermute | solution.py:59
  8.2 3.4 %copy-start.3 = (bf16[1,4096,256]{2,1,0:T(8,128)(2,1)S(1)}, bf16[1,4096,256]{2,1,0:T(8,128)(2,1)}, u32[]{:S(2)}) copy-start(bf16[1,4096,256]{2,1,0:T(8,128)(2,1)} %param.8) | copy-start | bytes 6291460
  9.1 5.2 %copy-start.6 = (f32[1,256,32]{1,2,0:T(8,128)S(1)}, f32[1,256,32]{1,2,0:T(8,128)}, u32[]{:S(2)}) copy-start(f32[1,256,32]{1,2,0:T(8,128)} %param.11) | copy-start | bytes 98308
  9.1 6.1 %copy-start.1 = (bf16[1,256,4096]{2,1,0:T(8,128)(2,1)S(1)}, bf16[1,256,4096]{2,1,0:T(8,128)(2,1)}, u32[]{:S(2)}) copy-start(bf16[1,256,4096]{2,1,0:T(8,128)(2,1)} %param.6) | copy-start | bytes 6291460
  11.7 18.1 %copy-start.5 = (f32[1,4096]{1,0:T(1,128)S(1)}, f32[1,4096]{1,0:T(1,128)}, u32[]{:S(2)}) copy-start(f32[1,4096]{1,0:T(1,128)} %param.7) | copy-start | bytes 49156
  15.3 55.6 %collective-permute-start.4 = (bf16[256,4096]{1,0:T(8,128)(2,1)S(1)}, bf16[256,4096]{1,0:T(8,128)(2,1)}, u32[]{:S(2)}, u32[]{:S(2)}) collective-permute-start(bf16[256,4096]{1,0:T(8,128)(2,1)S(1)} %bitcast.98), channel_id=1, source_target_pairs={{0,1},{1,0},{2,3},{3,2},{4,5},{5,4},{6,7},{7,6},{8,9},{9,8},{10,11... | collective-permute-start | bytes 6291464 | tf_op jit(solution)/shard_map/ppermute | solution.py:65
  37.3 5.6 %copy-start.7 = (f32[256]{0:T(256)S(1)}, f32[256]{0:T(256)}, u32[]{:S(2)}) copy-start(f32[256]{0:T(256)} %get-tuple-element.11) | copy-start | bytes 3076
  38.5 14.1 %all-to-all-start = ((f32[4,64,1024]{2,1,0:T(8,128)}), f32[4,64,1024]{2,1,0:T(8,128)S(1)}, u32[]{:S(2)}, u32[]{:S(2)}) async-start(f32[4,64,1024]{2,1,0:T(8,128)} %bitcast.102), calls=%async_computation | async-start | bytes 2097152 | tf_op jit(solution)/shard_map/all_to_all | solution.py:27
  55.2 17.8 %all-to-all-start.1 = ((f32[8,64,128]{2,1,0:T(8,128)}), f32[8,64,128]{2,1,0:T(8,128)S(1)}, u32[]{:S(2)}, u32[]{:S(2)}) async-start(f32[8,64,128]{2,1,0:T(8,128)} %copy.22), calls=%async_computation.1 | async-start | bytes 524288 | tf_op jit(solution)/shard_map/all_to_all | solution.py:27
  68.2 66.7 %collective-permute-start.3 = (bf16[256,4096]{1,0:T(8,128)(2,1)}, bf16[256,4096]{1,0:T(8,128)(2,1)}, u32[]{:S(2)}, u32[]{:S(2)}) collective-permute-start(bf16[256,4096]{1,0:T(8,128)(2,1)} %fusion.8), channel_id=1, source_target_pairs={{2,0},{3,1},{6,4},{7,5},{10,8},{11,9},{14,12},{15,13},{18,16},{19,... | collective-permute-start | bytes 6291464 | tf_op jit(solution)/shard_map/ppermute | solution.py:146
  73.6 8.5 %all-to-all-start.2 = ((f32[4,32,128]{2,1,0:T(8,128)}), f32[4,32,128]{2,1,0:T(8,128)S(1)}, u32[]{:S(2)}, u32[]{:S(2)}) async-start(f32[4,32,128]{2,1,0:T(8,128)} %bitcast.12), calls=%async_computation.2 | async-start | bytes 131072 | tf_op jit(solution)/shard_map/all_to_all | solution.py:27
  82.8 14.6 %all-to-all-start.3 = ((f32[8,32,128]{2,1,0:T(8,128)}), f32[8,32,128]{2,1,0:T(8,128)S(1)}, u32[]{:S(2)}, u32[]{:S(2)}) async-start(f32[8,32,128]{2,1,0:T(8,128)} %broadcast_in_dim.55), calls=%async_computation.3 | async-start | bytes 262144 | tf_op jit(solution)/shard_map/all_to_all | solution.py:27
  98.2 10.4 %all-to-all-start.4 = ((f32[4,32,1024]{2,1,0:T(8,128)}), f32[4,32,1024]{2,1,0:T(8,128)S(1)}, u32[]{:S(2)}, u32[]{:S(2)}) async-start(f32[4,32,1024]{2,1,0:T(8,128)} %broadcast_in_dim.57), calls=%async_computation.4 | async-start | bytes 1048576 | tf_op jit(solution)/shard_map/all_to_all | solution.py:27
  101.9 7.5 %copy-start.4 = (bf16[256,4096]{1,0:T(8,128)(2,1)S(1)}, bf16[256,4096]{1,0:T(8,128)(2,1)}, u32[]{:S(2)}) copy-start(bf16[256,4096]{1,0:T(8,128)(2,1)} %get-tuple-element.12) | copy-start | bytes 6291460
  109.4 3.4 %copy-start.2 = (bf16[1,4096,256]{2,1,0:T(8,128)(2,1)S(1)}, bf16[1,4096,256]{2,1,0:T(8,128)(2,1)}, u32[]{:S(2)}) copy-start(bf16[1,4096,256]{2,1,0:T(8,128)(2,1)} %param.10) | copy-start | bytes 6291460
  113.9 11.7 %all-to-all-start.5 = ((f32[8,32,256]{2,1,0:T(8,128)}), f32[8,32,256]{2,1,0:T(8,128)S(1)}, u32[]{:S(2)}, u32[]{:S(2)}) async-start(f32[8,32,256]{2,1,0:T(8,128)} %broadcast_in_dim.59), calls=%async_computation.5 | async-start | bytes 524288 | tf_op jit(solution)/shard_map/all_to_all | solution.py:27
  126.4 13.5 %all-to-all-start.6 = ((f32[8,32,256]{2,1,0:T(8,128)}), f32[8,32,256]{2,1,0:T(8,128)S(1)}, u32[]{:S(2)}, u32[]{:S(2)}) async-start(f32[8,32,256]{2,1,0:T(8,128)} %broadcast_in_dim.60), calls=%async_computation.6 | async-start | bytes 524288 | tf_op jit(solution)/shard_map/all_to_all | solution.py:27
  140.8 1.4 collective-permute-start.5
  143.4 2.4 %collective-permute-start.6 = (f32[1,1]{1,0:T(1,128)}, f32[1,1]{1,0:T(1,128)}, u32[]{:S(2)}, u32[]{:S(2)}) collective-permute-start(f32[1,1]{1,0:T(1,128)} %add.85), channel_id=1, source_target_pairs={{0,1},{1,0},{2,3},{3,2},{4,5},{5,4},{6,7},{7,6},{8,9},{9,8},{10,11... | collective-permute-start | bytes 20 | tf_op jit(solution)/shard_map/ppermute | solution.py:136

commit v2 on v0

v2 whole, which is shorter than its diff:
```python
import functools
import math

import jax
import jax.numpy as jnp
from jax import lax
from jax.experimental import pallas as pl
from jax.experimental.pallas import tpu as pltpu
from jax.sharding import Mesh, PartitionSpec as P

epsilon = 1e-05
clip_level = 0.25
DP = ("z", "y", "xh")
f32 = jnp.float32
bf16 = jnp.bfloat16
WIRE = f32
SWAP = [(0, 1), (1, 0)]
LIMIT = 60 * 1024 * 1024


def dot(left, right, left_dim, right_dim, precision=None):
    return lax.dot_general(
        left,
        right,
        (((left_dim,), (right_dim,)), ((), ())),
        precision=precision,
        preferred_element_type=f32,
    )


def exact(left, right, left_dim, right_dim):
    return dot(left, right, left_dim, right_dim, lax.Precision.HIGHEST)


def pieces(value, count):
    found = []
    for _ in range(count - 1):
        part = value.astype(bf16)
        found.append(part)
        value = value - part.astype(f32)
    found.append(value.astype(bf16))
    return found


def exchange(chunks, axis):
    return lax.all_to_all(chunks, axis, 0, 0, tiled=False)


def added(terms):
    return terms.astype(f32).sum(0).astype(terms.dtype)


class Stream:
    def __init__(self, far, near, done, dim, parts, begin=0):
        self.far, self.near, self.done, self.dim, self.parts = far, near, done, dim, parts
        self.size = near.shape[dim] // parts
        self.begin = begin
        self.waited = set()

    def place(self, part, begin=0):
        return (slice(None),) * self.dim + (pl.ds(begin + part * self.size, self.size),)

    def bring(self, part):
        source = self.far.at[self.place(part, self.begin)]
        return pltpu.make_async_copy(source, self.near.at[self.place(part)], self.done.at[part])

    def send(self, part):
        place = self.place(part)
        return pltpu.make_async_copy(self.near.at[place], self.far.at[place], self.done.at[part])

    def __call__(self, part=0):
        if part not in self.waited:
            self.bring(part).wait()
            self.waited.add(part)
        return self.near.at[self.place(part)]

    def all(self):
        for part in range(self.parts):
            self(part)
        return self.near

    def out(self, part=0):
        return self.near.at[self.place(part)]


def call(kernel, ins, outs, scratch=(), scalar=None, limit=LIMIT):
    n_in, n_out = len(ins), len(outs)
    scalars = [] if scalar is None else [scalar]

    def body(*refs):
        refs = list(refs)
        front = [refs.pop(0)[0] for _ in scalars]
        far, refs = refs[: n_in + n_out], refs[n_in + n_out :]
        own, refs = refs[: len(scratch)], refs[len(scratch) :]
        near, done = refs[: n_in + n_out], refs[n_in + n_out :]
        marks = [item[1:4] for item in ins]
        marks += [(dim, parts) for _, _, dim, parts in outs]
        streams = [Stream(*item, *mark) for *item, mark in zip(far, near, done, marks)]
        sources, targets = streams[:n_in], streams[n_in:]
        for part in range(max(source.parts for source in sources)):
            for source in sources:
                if part < source.parts:
                    source.bring(part).start()
        kernel(*front, *sources, *targets, *own)
        for source in sources:
            source.all()
        for target in targets:
            for part in range(target.parts):
                target.send(part).wait()

    shapes = []
    for array, dim, parts, *cut in ins:
        shape = list(array.shape)
        if cut:
            shape[dim] = cut[1]
        shapes.append((tuple(shape), array.dtype, parts))
    shapes += [(shape, dtype, parts) for shape, dtype, _, parts in outs]
    found = pl.pallas_call(
        body,
        out_shape=tuple(jax.ShapeDtypeStruct(shape, dtype) for shape, dtype, _, _ in outs),
        in_specs=[pl.BlockSpec(memory_space=pltpu.SMEM) for _ in scalars]
        + [pl.BlockSpec(memory_space=pl.ANY) for _ in ins],
        out_specs=tuple(pl.BlockSpec(memory_space=pl.ANY) for _ in outs),
        scratch_shapes=list(scratch)
        + [pltpu.VMEM(shape, dtype) for shape, dtype, _ in shapes]
        + [pltpu.SemaphoreType.DMA((parts,)) for _, _, parts in shapes],
        compiler_params=pltpu.CompilerParams(vmem_limit_bytes=limit),
        cost_estimate=pl.CostEstimate(flops=0, bytes_accessed=0, transcendentals=0),
    )(*scalars, *[item[0] for item in ins])
    return found if n_out > 1 else found[0]


def normed_of(rows, inverse, gain):
    return (rows * inverse * gain).astype(bf16)


def inverse_of(rows):
    return lax.rsqrt(jnp.mean(rows * rows, axis=-1, keepdims=True) + epsilon)


def half(shard, size):
    return pl.ds(pl.multiple_of(shard * size, size), size)


def projected_kernel(shard, upstream, basis, own_out, give_out, rows_out):
    rank, tokens = own_out.near.shape
    upstream()
    rows_out.near = upstream.near.at[half(1 - shard, tokens)]
    rows_out.send(0).start()
    parts = jnp.concatenate(pieces(basis()[...], 2), axis=0)
    for out, side in ((give_out, 1 - shard), (own_out, shard)):
        both = dot(parts, upstream()[half(side, tokens), :], 1, 1)
        out.out()[...] = both[:rank] + both[rank:]
        out.send(0).start()


def terms_kernel(shard, activ, gain, error, basis, own_v, other_v, normed, out):
    rank = basis.near.shape[0]
    lanes = out.near.shape[-1]
    for part in range(activ.parts):
        rows = activ(part)[...].astype(f32)
        normed.out(part)[...] = normed_of(rows, inverse_of(rows), gain()[...])
        normed.send(part).start()
    pair = jnp.concatenate(pieces(basis()[...], 2), axis=0)
    both = jnp.concatenate([own_v()[...], other_v()[...]], axis=0)
    both = jnp.concatenate(pieces(both, 2), axis=0)
    for part in range(error.parts):
        columns = slice(part * error.size, (part + 1) * error.size)
        product = dot(both, normed.near[:, columns], 1, 0)
        product = product[: 2 * rank] + product[2 * rank :]
        from_error = dot(pair, error(part)[...], 1, 1)
        own = product[:rank] + (from_error[:rank] + from_error[rank:])
        other = product[rank:]
        for chunk in range(out.size):
            columns = slice(chunk * lanes, (chunk + 1) * lanes)
            out.out(part)[chunk, shard] = own[:, columns].astype(out.near.dtype)
            out.out(part)[chunk, 1 - shard] = other[:, columns].astype(out.near.dtype)
        out.send(part).start()


def split_out(out, part, value):
    high, low = pieces(value, 2)
    columns = value.shape[1]
    out.out(part)[:, :columns] = high
    out.out(part)[:, columns:] = low
    out.send(part).start()


def joined(both):
    columns = both.shape[1] // 2
    return both[:, :columns].astype(f32) + both[:, columns:].astype(f32)


def own_kernel(shard, normed, upstream, error, out):
    rows = upstream()[half(shard, normed.near.shape[0]), :]
    for part in range(out.parts):
        split_out(out, part, dot(normed(part)[...], rows, 0, 0) + error(part)[...].astype(f32))


def merged_kernel(shard, activ, gain, upstream, own, out, inverse):
    rows = upstream()[half(1 - shard, activ.near.shape[0]), :]
    for part in range(activ.parts):
        place = pl.ds(part * activ.size, activ.size)
        inverse[place, :] = inverse_of(activ(part)[...].astype(f32))
    for part in range(out.parts):
        lanes = slice(part * out.size, (part + 1) * out.size)
        other = normed_of(activ.near[:, lanes].astype(f32), inverse[...], gain()[:, lanes])
        split_out(out, part, dot(other, rows, 0, 0) + joined(own(part)[...]))


def right_kernel(summed, merged, right_out, gram_out):
    rank = summed.near.shape[1]
    columns = merged.near.shape[1] // 2
    gram = right = 0.0
    for part in range(summed.parts):
        chunk = summed(part)
        whole = jnp.concatenate([chunk[i].astype(f32) for i in range(summed.size)], axis=1)
        parts = jnp.concatenate(pieces(whole, 3), axis=0)
        gram = gram + dot(parts, parts, 1, 1)
        right = right + dot(parts, merged(part)[...], 1, 0)
    right = right[:, :columns] + right[:, columns:]
    right = right[:rank] + right[rank : 2 * rank] + right[2 * rank :]
    right_out.out()[...] = jnp.broadcast_to(right[None], right_out.near.shape)
    right_out.send(0).start()
    gram = gram[:rank] + gram[rank : 2 * rank] + gram[2 * rank :]
    gram_out.out()[...] = gram[:, :rank] + gram[:, rank : 2 * rank] + gram[:, 2 * rank :]
    gram_out.send(0).start()


def left_kernel(gram, summed, left_out, parts_out, inverse_out, inverse):
    rank = gram.near.shape[0]
    row = lax.broadcasted_iota(jnp.int32, (rank, rank), 0)
    column = lax.broadcasted_iota(jnp.int32, (rank, rank), 1)
    both = jnp.concatenate([gram()[...], jnp.where(row == column, 1.0, 0.0)], axis=1)
    below = lax.broadcasted_iota(jnp.int32, (rank, 1), 0)
    for k in range(rank):
        scale = lax.rsqrt(both[k : k + 1, k : k + 1])
        pivot = both[k : k + 1, :] * scale
        inverse[k : k + 1, :] = pivot[:, rank:]
        factor = jnp.where(below > k, both[:, k : k + 1] * scale, 0.0)
        both = both - factor * pivot
    inverse_out.out()[...] = inverse[...]
    inverse_out.send(0).start()
    lanes = summed.near.shape[2] * summed.size
    for part in range(summed.parts):
        chunk = summed(part)
        whole = jnp.concatenate([chunk[i].astype(f32) for i in range(summed.size)], axis=1)
        left = exact(inverse[...], whole, 1, 0)
        left_out.out(part)[...] = left
        left_out.send(part).start()
        high, low = pieces(left, 2)
        parts_out.out(part)[...] = jnp.concatenate([high, low, high, high], axis=0).T
        parts_out.send(part).start()


def mean_kernel(terms, inverse, mean_out, parts_out, squares_out, *, replicas):
    total = jnp.sum(terms()[...], axis=0)
    mean = exact(inverse()[...], total, 1, 0) * (1.0 / replicas)
    squares = jnp.sum(jnp.sum(mean * mean, axis=1, keepdims=True), axis=0, keepdims=True)
    squares_out.out()[...] = jnp.broadcast_to(squares, squares_out.near.shape)
    squares_out.send(0).start()
    high, low = pieces(mean, 2)
    parts_out.out()[...] = jnp.concatenate([high, high, low, jnp.zeros_like(low)], axis=0)
    parts_out.send(0).start()
    mean_out.out()[...] = mean
    mean_out.send(0).start()


def error_kernel(merged, left, right, out):
    few = 128
    for part in range(out.parts):
        for start in range(0, out.size, few):
            rows = slice(start, start + few)
            approx = dot(left(part)[rows, :], right()[...], 1, 0)
            out.out(part)[rows, :] = (joined(merged(part)[rows, :]) - approx).astype(bf16)
        out.send(part).start()


def section_kernel(shard, activ, gain, upstream, other, weights, beside, *refs):
    out, scaled = refs
    tokens, width = activ.near.shape
    own = upstream()[half(shard, tokens), :]
    squares = along = 0.0
    for part in range(weights.parts):
        lanes = slice(part * weights.size, (part + 1) * weights.size)
        rows = activ()[:, lanes].astype(f32)
        product = dot(own, weights(part)[...], 1, 1) + dot(other()[...], beside(part)[...], 1, 1)
        product = product * gain()[:, lanes]
        scaled[:, lanes] = product
        squares = squares + jnp.sum(rows * rows, axis=-1, keepdims=True)
        along = along + jnp.sum(rows * product, axis=-1, keepdims=True)
    inverse = lax.rsqrt(squares * (1.0 / width) + epsilon)
    along = along * (1.0 / width) * inverse * inverse * inverse
    few = tokens // out.parts
    for part in range(out.parts):
        rows = slice(part * few, (part + 1) * few)
        value = inverse[rows] * scaled[rows, :] - activ()[rows, :].astype(f32) * along[rows]
        out.out(part)[...] = value.astype(bf16)
        out.send(part).start()


def local(activations, norm_gain, value_weight, upstream_grad, error_buffer, prior_basis):
    activ_own = activations[0]
    weights = value_weight[0]
    upstream = upstream_grad[0]
    error = error_buffer[0]
    basis = prior_basis[0].T
    tokens, width = activ_own.shape
    replica_tokens, columns = upstream.shape
    rank = basis.shape[0]
    shard = lax.axis_index("tensor")
    where = shard.astype(jnp.int32).reshape(1)
    n_y, n_z, n_x = lax.axis_size("y"), lax.axis_size("z"), lax.axis_size("xh")
    n_t, n_p = lax.axis_size("tensor"), lax.axis_size("pipe")
    replicas = n_y * n_z * n_x
    lanes = width // (n_z * n_y)
    steps = 8

    own_v, give_v, up_give = call(
        projected_kernel,
        [(upstream, 0, 1), (basis, 0, 1)],
        [((rank, tokens), f32, 0, 1)] * 2 + [((tokens, columns), bf16, 0, 1)],
        scalar=where,
    )
    other_v = lax.ppermute(give_v, "tensor", SWAP)
    up_other = lax.ppermute(up_give, ("pipe", "tensor"), [(2, 3), (3, 2)])

    other_v, up_other, activ_late, weights_late = lax.optimization_barrier(
        (other_v, up_other, activ_own, weights)
    )
    activ_other = lax.ppermute(activ_late, "tensor", SWAP)
    beside = [(2, 7), (7, 2), (3, 6), (6, 3)]
    weights_other = lax.ppermute(weights_late, ("xh", "pipe", "tensor"), beside)
    normed_own, terms = call(
        terms_kernel,
        [
            (activ_late, 0, 4),
            (norm_gain, 0, 1),
            (error, 0, 4),
            (basis, 0, 1),
            (own_v, 0, 1),
            (other_v, 0, 1),
        ],
        [((tokens, width), bf16, 0, 4), ((n_y * n_z, n_t, rank, lanes), WIRE, 0, 4)],
        scalar=where,
    )
    terms = terms.reshape(n_y * n_z, n_t * rank, lanes)
    terms, activ_late, normed_late = lax.optimization_barrier((terms, activ_own, normed_own))
    terms = exchange(terms, ("y", "z"))
    section_grad = call(
        section_kernel,
        [
            (activ_late, 0, 1),
            (norm_gain, 0, 1),
            (upstream, 0, 1),
            (up_other, 0, 1),
            (weights, 0, steps),
            (weights_other, 0, steps),
        ],
        [((tokens, width), bf16, 0, 4)],
        scratch=[pltpu.VMEM((tokens, width), f32)],
        scalar=where,
    )
    own = call(
        own_kernel,
        [(normed_late, 1, 4), (upstream, 0, 1), (error, 0, 4)],
        [((width, 2 * columns), bf16, 0, 4)],
        scalar=where,
    )
    received = lax.ppermute(section_grad, "pipe", [(1, 0)])
    terms, activ_other, own = lax.optimization_barrier((terms, activ_other, own))
    terms = added(terms).reshape(1, n_t, rank, lanes)
    terms = jnp.broadcast_to(terms, (n_x, n_t, rank, lanes)).reshape(n_x * n_t, rank, lanes)
    summed = added(exchange(terms, ("xh", "tensor")))
    summed = exchange(jnp.broadcast_to(summed[None], (n_z,) + summed.shape), "z")
    summed, received, own = lax.optimization_barrier((summed, received, own))
    summed = exchange(jnp.broadcast_to(summed[None], (n_y,) + summed.shape), "y")
    merged = call(
        merged_kernel,
        [
            (activ_other, 0, 4),
            (norm_gain, 0, 1),
            (upstream, 0, 1),
            (own, 0, 4),
        ],
        [((width, 2 * columns), bf16, 0, 4)],
        scratch=[pltpu.VMEM((tokens, 1), f32)],
        scalar=where,
    )
    summed, merged = lax.optimization_barrier((summed, merged))
    summed = summed.reshape(n_y * n_z, rank, lanes)
    near = n_y * n_x
    right_terms, gram = call(
        right_kernel,
        [(summed, 0, 4), (merged, 0, 4)],
        [((near, rank, columns), f32, 0, 1), ((rank, rank), f32, 0, 1)],
    )
    right_terms = exchange(right_terms, ("y", "xh"))
    left, left_parts, inverse = call(
        left_kernel,
        [(gram, 0, 1), (summed, 0, 4)],
        [
            ((rank, width), f32, 1, 4),
            ((width, 4 * rank), bf16, 0, 4),
            ((rank, rank), f32, 0, 1),
        ],
        scratch=[pltpu.VMEM((rank, rank), f32)],
    )
    right_terms, left, left_parts, inverse, received = lax.optimization_barrier(
        (right_terms, left, left_parts, inverse, received)
    )
    last = lax.axis_index("pipe") == n_p - 1
    received = jnp.where(last, jnp.zeros_like(received), received)
    right_terms = jnp.broadcast_to(right_terms.sum(0)[None], (n_z, rank, columns))
    right_terms = exchange(right_terms, "z")
    right_terms, received = lax.optimization_barrier((right_terms, received))
    mean_right, right_parts, squares = call(
        functools.partial(mean_kernel, replicas=replicas),
        [(right_terms, 0, 1), (inverse, 0, 1)],
        [
            ((rank, columns), f32, 0, 1),
            ((4 * rank, columns), bf16, 0, 1),
            ((rank, columns), f32, 0, 1),
        ],
        limit=8 * 1024 * 1024,
    )
    total = (
        squares
        + lax.ppermute(squares, "pipe", SWAP)
        + lax.ppermute(squares, "tensor", SWAP)
        + lax.ppermute(squares, ("pipe", "tensor"), [(0, 3), (3, 0), (1, 2), (2, 1)])
    )
    error_next = call(
        error_kernel,
        [
            (merged, 0, 4),
            (left_parts, 0, 4),
            (right_parts, 0, 1),
        ],
        [((width, columns), bf16, 0, 4)],
    )
    entries = mean_right.size * n_p * n_t
    factor = jnp.minimum(1.0, clip_level * math.sqrt(entries) / jnp.sqrt(total + 1e-06))
    return (
        received[None],
        left.T[None],
        (mean_right * factor).T[None],
        error_next[None],
    )


def solution(mesh):
    inner = Mesh(
        mesh.devices.reshape((8, 4, 2, mesh.shape["pipe"], mesh.shape["tensor"])),
        DP + ("pipe", "tensor"),
    )
    return jax.shard_map(
        local,
        mesh=inner,
        in_specs=(
            P("pipe", DP + ("tensor",), None),
            P("pipe", None),
            P("pipe", None, "tensor"),
            P("pipe", DP, "tensor"),
            P("pipe", DP, "tensor"),
            P("pipe", "tensor", None),
        ),
        out_specs=(
            P("pipe", DP + ("tensor",), None),
            P("pipe", "tensor", None),
            P("pipe", "tensor", None),
            P("pipe", DP, "tensor"),
        ),
        check_vma=False,
    )
```

time: 1300 us -> 139 us (0.11)
  waiting for transfers between devices: 817 us -> 25.5 us
  blocking collectives: 409 us -> 22.9 us
  Pallas kernels: 0 us -> 42.2 us
  starting transfers between devices: 4.03 us -> 40.3 us
  matrix products: 28.7 us -> 0 us
  between operations: 14.5 us -> 0.85 us
  other arithmetic: 15.7 us -> 2.19 us
    psum x1 -> x0, waiting for transfers between devices: 649 us -> none  [local(): summed = lax.psum(local_left, 'dp')]
    psum x2 -> x0, blocking collectives: 409 us -> none  [the longest x1 301 us: local(): mean_right = lax.psum(local_right, 'dp') / replicas]
    reduce_scatter x1 -> x0, waiting for transfers between devices: 108 us -> none  [local(): lax.psum_scatter(lax.dot_general(matching, weights, (((1,), (1,)), ((), (...]
    all_gather x1 -> x0, waiting for transfers between devices: 59 us -> none  [local(): lax.all_gather(normed, 'tensor', axis=0, tiled=True)]
    pallas_call x0 -> x9, Pallas kernels: none -> 42.2 us  [call(): pl.pallas_call(body, out_shape=tuple((jax.ShapeDtypeStruct(shape, dtype)...]
    dot_general x6 -> x0, matrix products: 27 us -> none  [the longest x1 6.26 us: local(): lax.dot_general(left, mean_right, (((1,), (1,)), ((), ())), precision=lax...]
    all_to_all x0 -> x4, starting transfers between devices: none -> 23.1 us  [exchange(): return lax.all_to_all(chunks, axis, 0, 0, tiled=False)]
    all_to_all x0 -> x2, blocking collectives: none -> 22.9 us  [exchange(): return lax.all_to_all(chunks, axis, 0, 0, tiled=False)]
  transfers between devices with their start and end apart: 4 -> 12, of which waited for: 3 -> 7; matrix products, arithmetic and copies ran while one was open for 1% -> 1% of each run, Pallas kernels for 0% -> 26%
where the time goes in v2:
time: 139 us; the launch traced here: 138 us
  Pallas kernels  42.2 us (30%)
  starting transfers between devices  40.3 us (29%)
  waiting for transfers between devices  25.5 us (18%)
  blocking collectives  22.9 us (16%)
  local copies, waits for them, and re-layouts  4.37 us (3%)
  other arithmetic  2.19 us (2%)
    pallas_call x9, Pallas kernels, call(): pl.pallas_call(body, out_shape=tuple((jax.ShapeDtypeStruct(shape, dtype)...  42.2 us
    all_to_all x4, starting transfers between devices, exchange(): return lax.all_to_all(chunks, axis, 0, 0, tiled=False)  23.1 us
    all_to_all x2, blocking collectives, exchange(): return lax.all_to_all(chunks, axis, 0, 0, tiled=False)  22.9 us
    all_to_all x4, waiting for transfers between devices, exchange(): return lax.all_to_all(chunks, axis, 0, 0, tiled=False)  13.4 us
    ppermute x1, waiting for transfers between devices, local(): weights_other = lax.ppermute(weights_late, ('xh', 'pipe', 'tensor'), beside)  7.39 us
    ppermute x1, starting transfers between devices, local(): lax.ppermute(squares, 'pipe', SWAP)  5.1 us
    ppermute x1, starting transfers between devices, local(): weights_other = lax.ppermute(weights_late, ('xh', 'pipe', 'tensor'), beside)  4.82 us
    ppermute x1, starting transfers between devices, local(): up_other = lax.ppermute(up_give, ('pipe', 'tensor'), [(2, 3), (3, 2)])  3.95 us
  transfers between devices with their start and end apart: 12, of which 7 were waited for; matrix products, arithmetic and copies ran while one was open for 1% of the time, Pallas kernels for 26%

profile of v2, /device:TPU:1, one launch (start us, length us, event | category | flops | bytes accessed | tf_op | source)
XLA Modules:
  0.0 138.3 jit_solution(14580111348554283999)
XLA Ops:
  0.6 1.8 %shard_map.93 = (f32[32,256]{1,0:T(8,128)}, f32[32,256]{1,0:T(8,128)}, bf16[256,256]{1,0:T(8,128)(2,1)}) custom-call(s32[1]{0:T(128)} %bitcast.refs_0_, bf16[512,256]{1,0:T(8,128)(2,1)} %bitcast.28, f32[32,256]{1,0:T(8,128)} %bitcast.38), custom_call_target="tpu_custom_call" | custom-call | tf_op jit(solution)/shard_map/pallas_call | solution.py:118
  2.5 3.9 %collective-permute-start.1 = (bf16[256,256]{1,0:T(8,128)(2,1)}, bf16[256,256]{1,0:T(8,128)(2,1)S(1)}, u32[]{:S(2)}, u32[]{:S(2)}) collective-permute-start(bf16[256,256]{1,0:T(8,128)(2,1)} %get-tuple-element.40), channel_id=1, source_target_pairs={{2,3},{3,2},{6,7},{7,6},{10,11},{11,10},{14,15},{15,14},{18,19},{1... | collective-permute-start | bytes 393224 | tf_op jit(solution)/shard_map/ppermute | solution.py:326
  6.4 0.1 collective-permute-start
  6.5 3.0 %collective-permute-done.refs_6_ = f32[32,256]{1,0:T(8,128)S(1)} collective-permute-done((f32[32,256]{1,0:T(8,128)}, f32[32,256]{1,0:T(8,128)S(1)}, u32[]{:S(2)}, u32[]{:S(2)}) %collective-permute-start) | collective-permute-done | bytes 32800 | tf_op jit(solution)/shard_map/ppermute | solution.py:325
  9.5 0.0 collective-permute-done.1.refs_4_
  9.5 4.8 %collective-permute-start.3 = (bf16[4096,256]{1,0:T(8,128)(2,1)}, bf16[4096,256]{1,0:T(8,128)(2,1)S(1)}, u32[]{:S(2)}, u32[]{:S(2)}) collective-permute-start(bf16[4096,256]{1,0:T(8,128)(2,1)} %bitcast.32), channel_id=1, source_target_pairs={{2,7},{7,2},{3,6},{6,3},{10,15},{15,10},{11,14},{14,11},{18,23},{2... | collective-permute-start | bytes 6291464 | tf_op jit(solution)/shard_map/ppermute | solution.py:333
  14.3 0.1 collective-permute-start.2
  14.4 0.0 copy-done.5
  14.4 5.2 %shard_map.94 = (bf16[256,4096]{1,0:T(8,128)(2,1)}, f32[32,2,32,128]{3,2,1,0:T(8,128)}) custom-call(s32[1]{0:T(128)} %bitcast.refs_0_, bf16[256,4096]{1,0:T(8,128)(2,1)} %bitcast.24, f32[1,4096]{1,0:T(1,128)} %refs_2_.5, bf16[4096,256]{1,0:T(8,128)(2,1)} %bitcast.21, f32[32,256]{1,0:T(8,128)} %bitcast.39, f32[32,256]{1,0:T(8,128)} %get-tuple-element.42.refs_5_, ...), custom_call_target="tpu_custom_call" | custom-call | tf_op jit(solution)/shard_map/pallas_call | solution.py:118
  19.6 0.0 copy-done.4
  19.6 11.2 %all-to-all-start = ((f32[32,64,128]{2,1,0:T(8,128)}), f32[32,64,128]{2,1,0:T(8,128)S(1)}, u32[]{:S(2)}, u32[]{:S(2)}) async-start(f32[32,64,128]{2,1,0:T(8,128)} %bitcast.36), calls=%async_computation | async-start | bytes 2097152 | tf_op jit(solution)/shard_map/all_to_all | solution.py:46
  30.9 7.4 %collective-permute-done.3.refs_6_ = bf16[4096,256]{1,0:T(8,128)(2,1)S(1)} collective-permute-done((bf16[4096,256]{1,0:T(8,128)(2,1)}, bf16[4096,256]{1,0:T(8,128)(2,1)S(1)}, u32[]{:S(2)}, u32[]{:S(2)}) %collective-permute-start.3) | collective-permute-done | bytes 2097184 | tf_op jit(solution)/shard_map/ppermute | solution.py:333
  38.2 1.3 copy-done.3
  39.6 8.6 %shard_map.96 = bf16[256,4096]{1,0:T(8,128)(2,1)} custom-call(s32[1]{0:T(128)} %bitcast.refs_0_, bf16[256,4096]{1,0:T(8,128)(2,1)} %bitcast.25, f32[1,4096]{1,0:T(1,128)} %refs_2_.5, bf16[512,256]{1,0:T(8,128)(2,1)} %bitcast.29, bf16[256,256]{1,0:T(8,128)(2,1)} %copy-done.4, bf16[4096,256]{1,0:T(8,128)(2,1)} %bitcast.33, bf16[4096,256]{1,0:T(8,128)(2,1)} %copy-done.3), custom_call_target="tpu_custom_call" | custom-call | tf_op jit(solution)/shard_map/pallas_call | solution.py:118
  48.2 1.4 %collective-permute-start.4 = (bf16[256,4096]{1,0:T(8,128)(2,1)}, bf16[256,4096]{1,0:T(8,128)(2,1)S(1)}, u32[]{:S(2)}, u32[]{:S(2)}) collective-permute-start(bf16[256,4096]{1,0:T(8,128)(2,1)} %shard_map.96), channel_id=1, source_target_pairs={{2,0},{3,1},{6,4},{7,5},{10,8},{11,9},{14,12},{15,13},{18,16},{19,... | collective-permute-start | bytes 6291464 | tf_op jit(solution)/shard_map/ppermute | solution.py:370
  49.6 5.0 %shard_map.95.refs_4_ = bf16[4096,512]{1,0:T(8,128)(2,1)} custom-call(s32[1]{0:T(128)} %bitcast.refs_0_, bf16[256,4096]{1,0:T(8,128)(2,1)} %get-tuple-element.47.refs_1_, bf16[512,256]{1,0:T(8,128)(2,1)} %bitcast.30, bf16[4096,256]{1,0:T(8,128)(2,1)} %bitcast.22), custom_call_target="tpu_custom_call" | custom-call | tf_op jit(solution)/shard_map/pallas_call | solution.py:118
  54.6 3.3 %all-to-all-done = f32[32,64,128]{2,1,0:T(8,128)S(1)} async-done(((f32[32,64,128]{2,1,0:T(8,128)}), f32[32,64,128]{2,1,0:T(8,128)S(1)}, u32[]{:S(2)}, u32[]{:S(2)}) %all-to-all-start) | async-done | bytes 1048608 | tf_op jit(solution)/shard_map/all_to_all | solution.py:46
  57.8 1.8 %collective-permute-done.2.refs_1_ = bf16[256,4096]{1,0:T(8,128)(2,1)} collective-permute-done((bf16[256,4096]{1,0:T(8,128)(2,1)}, bf16[256,4096]{1,0:T(8,128)(2,1)}, u32[]{:S(2)}, u32[]{:S(2)}) %collective-permute-start.2) | collective-permute-done | bytes 2097184 | tf_op jit(solution)/shard_map/ppermute | solution.py:331
  59.6 0.1 reduce_sum.27
  59.7 7.0 %all_to_all.30 = f32[4,32,128]{2,1,0:T(8,128)S(1)} all-to-all(f32[4,32,128]{2,1,0:T(8,128)S(1)} %bitcast.37), channel_id=1, replica_groups=mesh['z'=8,'y'=4,'xh'=2,'pipe'=2,'tensor'=2] {'xh','tensor'}, dimensions={0} | all-to-all | bytes 131072 | tf_op jit(solution)/shard_map/all_to_all | solution.py:46
  66.8 15.8 %all_to_all.31 = f32[8,32,128]{2,1,0:T(8,128)S(1)} all-to-all(f32[8,32,128]{2,1,0:T(8,128)S(1)} %broadcast_in_dim.42), channel_id=1, replica_groups=mesh['z'=8,'y'=4,'xh'=2,'pipe'=2,'tensor'=2] {'z'}, dimensions={0} | all-to-all | bytes 262144 | tf_op jit(solution)/shard_map/all_to_all | solution.py:46
  82.6 0.0 collective-permute-done.4
  82.6 0.9 broadcast_in_dim.43
  83.5 4.2 %all-to-all-start.3 = ((f32[4,8,32,128]{3,2,1,0:T(8,128)}), f32[4,8,32,128]{3,2,1,0:T(8,128)S(1)}, u32[]{:S(2)}, u32[]{:S(2)}) async-start(f32[4,8,32,128]{3,2,1,0:T(8,128)} %broadcast_in_dim.43), calls=%async_computation.3 | async-start | bytes 1048576 | tf_op jit(solution)/shard_map/all_to_all | solution.py:46
  87.6 6.5 %shard_map.97.refs_1_.refs_0_ = bf16[4096,512]{1,0:T(8,128)(2,1)} custom-call(s32[1]{0:T(128)} %bitcast.refs_0_, bf16[256,4096]{1,0:T(8,128)(2,1)} %collective-permute-done.2.refs_1_, f32[1,4096]{1,0:T(1,128)} %refs_2_.5, bf16[512,256]{1,0:T(8,128)(2,1)} %bitcast.31, bf16[4096,512]{1,0:T(8,128)(2,1)} %shard_map.95.refs_4_), custom_call_target="tpu_custom_call" | custom-call | tf_op jit(solution)/shard_map/pallas_call | solution.py:118
  94.2 0.4 all-to-all-done.3
  94.6 0.8 copy-done.2
  95.4 4.1 %shard_map.98 = (f32[8,32,256]{2,1,0:T(8,128)}, f32[32,32]{1,0:T(8,128)}) custom-call(f32[32,32,128]{2,1,0:T(8,128)} %bitcast.26, bf16[4096,512]{1,0:T(8,128)(2,1)} %shard_map.97.refs_1_.refs_0_), custom_call_target="tpu_custom_call" | custom-call | tf_op jit(solution)/shard_map/pallas_call | solution.py:118
  99.5 4.3 %all-to-all-start.4 = ((f32[8,32,256]{2,1,0:T(8,128)}), f32[8,32,256]{2,1,0:T(8,128)S(1)}, u32[]{:S(2)}, u32[]{:S(2)}) async-start(f32[8,32,256]{2,1,0:T(8,128)} %get-tuple-element.58), calls=%async_computation.4 | async-start | bytes 524288 | tf_op jit(solution)/shard_map/all_to_all | solution.py:46
  103.8 5.8 %shard_map.99 = (f32[32,4096]{1,0:T(8,128)}, bf16[4096,128]{1,0:T(8,128)(2,1)}, f32[32,32]{1,0:T(8,128)}) custom-call(f32[32,32]{1,0:T(8,128)} %get-tuple-element.59.refs_0_, f32[32,32,128]{2,1,0:T(8,128)} %bitcast.27), custom_call_target="tpu_custom_call" | custom-call | tf_op jit(solution)/shard_map/pallas_call | solution.py:118
  109.6 1.9 %all-to-all-done.4 = f32[8,32,256]{2,1,0:T(8,128)S(1)} async-done(((f32[8,32,256]{2,1,0:T(8,128)}), f32[8,32,256]{2,1,0:T(8,128)S(1)}, u32[]{:S(2)}, u32[]{:S(2)}) %all-to-all-start.4) | async-done | bytes 262176 | tf_op jit(solution)/shard_map/all_to_all | solution.py:46
  111.6 0.7 broadcast_in_dim.44
  112.3 3.4 %all-to-all-start.5 = ((f32[8,32,256]{2,1,0:T(8,128)}), f32[8,32,256]{2,1,0:T(8,128)S(1)}, u32[]{:S(2)}, u32[]{:S(2)}) async-start(f32[8,32,256]{2,1,0:T(8,128)} %broadcast_in_dim.44), calls=%async_computation.5 | async-start | bytes 524288 | tf_op jit(solution)/shard_map/all_to_all | solution.py:46
  115.7 0.0 copy-start.1
  115.7 1.5 %broadcast_select_fusion = bf16[256,4096]{1,0:T(8,128)(2,1)} fusion(bf16[256,4096]{1,0:T(8,128)(2,1)S(1)} %collective-permute-done.4, pred[]{:T(512)S(6)} %eq.3), kind=kLoop, calls=%fused_computation | loop fusion | flops 1048576 | bytes 4194305 | tf_op jit(solution)/shard_map/jit(_where)/select_n | solution.py:413
  117.2 7.8 %all-to-all-done.5.refs_0_ = f32[8,32,256]{2,1,0:T(8,128)S(1)} async-done(((f32[8,32,256]{2,1,0:T(8,128)}), f32[8,32,256]{2,1,0:T(8,128)S(1)}, u32[]{:S(2)}, u32[]{:S(2)}) %all-to-all-start.5) | async-done | bytes 262176 | tf_op jit(solution)/shard_map/all_to_all | solution.py:46
  125.0 0.0 copy-done.1
  125.0 0.5 shard_map.100
  125.5 0.0 copy-start
  125.5 0.6 copy-done
  126.1 5.1 %collective-permute-start.5 = (f32[32,256]{1,0:T(8,128)S(1)}, f32[32,256]{1,0:T(8,128)S(1)}, u32[]{:S(2)}, u32[]{:S(2)}) collective-permute-start(f32[32,256]{1,0:T(8,128)S(1)} %get-tuple-element.71), channel_id=1, source_target_pairs={{0,2},{2,0},{1,3},{3,1},{4,6},{6,4},{5,7},{7,5},{8,10},{10,8},{9,1... | collective-permute-start | bytes 98312 | tf_op jit(solution)/shard_map/ppermute | solution.py:429
  131.2 0.8 collective-permute-start.6
  132.0 0.9 collective-permute-start.7
  132.9 4.7 %shard_map.101 = bf16[4096,256]{1,0:T(8,128)(2,1)} custom-call(bf16[4096,512]{1,0:T(8,128)(2,1)} %shard_map.97.refs_1_.refs_0_, bf16[4096,128]{1,0:T(8,128)(2,1)} %get-tuple-element.72.refs_1_, bf16[128,256]{1,0:T(8,128)(2,1)} %copy-done), custom_call_target="tpu_custom_call" | custom-call | tf_op jit(solution)/shard_map/pallas_call | solution.py:118
  137.6 0.0 collective-permute-done.5
  137.6 0.0 collective-permute-done.6
  137.6 0.0 collective-permute-done.7
  137.6 0.6 multiply_bitcast_fusion
  (8 shorter events, 0.1 us)
Async XLA Ops:
  2.5 7.0 %collective-permute-start.1 = (bf16[256,256]{1,0:T(8,128)(2,1)}, bf16[256,256]{1,0:T(8,128)(2,1)S(1)}, u32[]{:S(2)}, u32[]{:S(2)}) collective-permute-start(bf16[256,256]{1,0:T(8,128)(2,1)} %get-tuple-element.40), channel_id=1, source_target_pairs={{2,3},{3,2},{6,7},{7,6},{10,11},{11,10},{14,15},{15,14},{18,19},{1... | collective-permute-start | bytes 393224 | tf_op jit(solution)/shard_map/ppermute | solution.py:326
  6.4 3.1 %collective-permute-start = (f32[32,256]{1,0:T(8,128)}, f32[32,256]{1,0:T(8,128)S(1)}, u32[]{:S(2)}, u32[]{:S(2)}) collective-permute-start(f32[32,256]{1,0:T(8,128)} %get-tuple-element.39), channel_id=1, source_target_pairs={{0,1},{1,0},{2,3},{3,2},{4,5},{5,4},{6,7},{7,6},{8,9},{9,8},{10,11... | collective-permute-start | bytes 98312 | tf_op jit(solution)/shard_map/ppermute | solution.py:325
  9.5 4.9 %copy-start.5 = (f32[32,256]{1,0:T(8,128)}, f32[32,256]{1,0:T(8,128)S(1)}, u32[]{:S(2)}) copy-start(f32[32,256]{1,0:T(8,128)S(1)} %collective-permute-done.refs_6_) | copy-start | bytes 98308
  9.5 10.1 %copy-start.4 = (bf16[256,256]{1,0:T(8,128)(2,1)}, bf16[256,256]{1,0:T(8,128)(2,1)S(1)}, u32[]{:S(2)}) copy-start(bf16[256,256]{1,0:T(8,128)(2,1)S(1)} %collective-permute-done.1.refs_4_) | copy-start | bytes 393220
  9.5 28.7 %collective-permute-start.3 = (bf16[4096,256]{1,0:T(8,128)(2,1)}, bf16[4096,256]{1,0:T(8,128)(2,1)S(1)}, u32[]{:S(2)}, u32[]{:S(2)}) collective-permute-start(bf16[4096,256]{1,0:T(8,128)(2,1)} %bitcast.32), channel_id=1, source_target_pairs={{2,7},{7,2},{3,6},{6,3},{10,15},{15,10},{11,14},{14,11},{18,23},{2... | collective-permute-start | bytes 6291464 | tf_op jit(solution)/shard_map/ppermute | solution.py:333
  14.3 45.3 %collective-permute-start.2 = (bf16[256,4096]{1,0:T(8,128)(2,1)}, bf16[256,4096]{1,0:T(8,128)(2,1)}, u32[]{:S(2)}, u32[]{:S(2)}) collective-permute-start(bf16[256,4096]{1,0:T(8,128)(2,1)} %bitcast.23), channel_id=1, source_target_pairs={{0,1},{1,0},{2,3},{3,2},{4,5},{5,4},{6,7},{7,6},{8,9},{9,8},{10,11... | collective-permute-start | bytes 6291464 | tf_op jit(solution)/shard_map/ppermute | solution.py:331
  19.6 38.2 %all-to-all-start = ((f32[32,64,128]{2,1,0:T(8,128)}), f32[32,64,128]{2,1,0:T(8,128)S(1)}, u32[]{:S(2)}, u32[]{:S(2)}) async-start(f32[32,64,128]{2,1,0:T(8,128)} %bitcast.36), calls=%async_computation | async-start | bytes 2097152 | tf_op jit(solution)/shard_map/all_to_all | solution.py:46
  38.2 1.3 copy-start.3
  48.2 34.4 %collective-permute-start.4 = (bf16[256,4096]{1,0:T(8,128)(2,1)}, bf16[256,4096]{1,0:T(8,128)(2,1)S(1)}, u32[]{:S(2)}, u32[]{:S(2)}) collective-permute-start(bf16[256,4096]{1,0:T(8,128)(2,1)} %shard_map.96), channel_id=1, source_target_pairs={{2,0},{3,1},{6,4},{7,5},{10,8},{11,9},{14,12},{15,13},{18,16},{19,... | collective-permute-start | bytes 6291464 | tf_op jit(solution)/shard_map/ppermute | solution.py:370
  83.5 11.1 %all-to-all-start.3 = ((f32[4,8,32,128]{3,2,1,0:T(8,128)}), f32[4,8,32,128]{3,2,1,0:T(8,128)S(1)}, u32[]{:S(2)}, u32[]{:S(2)}) async-start(f32[4,8,32,128]{3,2,1,0:T(8,128)} %broadcast_in_dim.43), calls=%async_computation.3 | async-start | bytes 1048576 | tf_op jit(solution)/shard_map/all_to_all | solution.py:46
  94.6 0.8 copy-start.2
  99.5 12.1 %all-to-all-start.4 = ((f32[8,32,256]{2,1,0:T(8,128)}), f32[8,32,256]{2,1,0:T(8,128)S(1)}, u32[]{:S(2)}, u32[]{:S(2)}) async-start(f32[8,32,256]{2,1,0:T(8,128)} %get-tuple-element.58), calls=%async_computation.4 | async-start | bytes 524288 | tf_op jit(solution)/shard_map/all_to_all | solution.py:46
  112.3 12.7 %all-to-all-start.5 = ((f32[8,32,256]{2,1,0:T(8,128)}), f32[8,32,256]{2,1,0:T(8,128)S(1)}, u32[]{:S(2)}, u32[]{:S(2)}) async-start(f32[8,32,256]{2,1,0:T(8,128)} %broadcast_in_dim.44), calls=%async_computation.5 | async-start | bytes 524288 | tf_op jit(solution)/shard_map/all_to_all | solution.py:46
  115.7 9.3 %copy-start.1 = (f32[32,32]{1,0:T(8,128)S(1)}, f32[32,32]{1,0:T(8,128)}, u32[]{:S(2)}) copy-start(f32[32,32]{1,0:T(8,128)} %get-tuple-element.69.refs_1_) | copy-start | bytes 12292
  125.5 0.7 copy-start
  126.1 11.5 %collective-permute-start.5 = (f32[32,256]{1,0:T(8,128)S(1)}, f32[32,256]{1,0:T(8,128)S(1)}, u32[]{:S(2)}, u32[]{:S(2)}) collective-permute-start(f32[32,256]{1,0:T(8,128)S(1)} %get-tuple-element.71), channel_id=1, source_target_pairs={{0,2},{2,0},{1,3},{3,1},{4,6},{6,4},{5,7},{7,5},{8,10},{10,8},{9,1... | collective-permute-start | bytes 98312 | tf_op jit(solution)/shard_map/ppermute | solution.py:429
  131.2 6.4 %collective-permute-start.6 = (f32[32,256]{1,0:T(8,128)S(1)}, f32[32,256]{1,0:T(8,128)S(1)}, u32[]{:S(2)}, u32[]{:S(2)}) collective-permute-start(f32[32,256]{1,0:T(8,128)S(1)} %get-tuple-element.71), channel_id=1, source_target_pairs={{0,1},{1,0},{2,3},{3,2},{4,5},{5,4},{6,7},{7,6},{8,9},{9,8},{10,11... | collective-permute-start | bytes 98312 | tf_op jit(solution)/shard_map/ppermute | solution.py:430
  132.0 5.6 %collective-permute-start.7 = (f32[32,256]{1,0:T(8,128)S(1)}, f32[32,256]{1,0:T(8,128)S(1)}, u32[]{:S(2)}, u32[]{:S(2)}) collective-permute-start(f32[32,256]{1,0:T(8,128)S(1)} %get-tuple-element.71), channel_id=1, source_target_pairs={{0,3},{3,0},{1,2},{2,1},{4,7},{7,4},{5,6},{6,5},{8,11},{11,8},{9,1... | collective-permute-start | bytes 98312 | tf_op jit(solution)/shard_map/ppermute | solution.py:431

commit v3 on v2

--- a/solution.py
+++ b/solution.py
@@ -372,9 +372,8 @@
     terms = added(terms).reshape(1, n_t, rank, lanes)
     terms = jnp.broadcast_to(terms, (n_x, n_t, rank, lanes)).reshape(n_x * n_t, rank, lanes)
     summed = added(exchange(terms, ("xh", "tensor")))
-    summed = exchange(jnp.broadcast_to(summed[None], (n_z,) + summed.shape), "z")
-    summed, received, own = lax.optimization_barrier((summed, received, own))
-    summed = exchange(jnp.broadcast_to(summed[None], (n_y,) + summed.shape), "y")
+    summed, own = lax.optimization_barrier((summed, own))
+    summed = exchange(jnp.broadcast_to(summed[None], (n_y * n_z,) + summed.shape), ("y", "z"))
     merged = call(
         merged_kernel,
         [
@@ -387,8 +386,7 @@
         scratch=[pltpu.VMEM((tokens, 1), f32)],
         scalar=where,
     )
-    summed, merged = lax.optimization_barrier((summed, merged))
-    summed = summed.reshape(n_y * n_z, rank, lanes)
+    summed, merged, received = lax.optimization_barrier((summed, merged, received))
     near = n_y * n_x
     right_terms, gram = call(
         right_kernel,

time: 139 us -> 138 us (level)
  blocking collectives: 22.9 us -> 7.03 us
  starting transfers between devices: 40.3 us -> 48.3 us
  waiting for transfers between devices: 25.5 us -> 32.6 us
    all_to_all x2 -> x1, blocking collectives: 22.9 us -> 7.03 us  [exchange(): return lax.all_to_all(chunks, axis, 0, 0, tiled=False)]
    all_to_all x4, starting transfers between devices: 23.1 us -> 32.3 us  [exchange(): return lax.all_to_all(chunks, axis, 0, 0, tiled=False)]
    all_to_all x4, waiting for transfers between devices: 13.4 us -> 20.5 us  [exchange(): return lax.all_to_all(chunks, axis, 0, 0, tiled=False)]
  transfers between devices with their start and end apart: 12 -> 12, of which waited for: 7 -> 7; matrix products, arithmetic and copies ran while one was open for 1% -> 2% of each run, Pallas kernels for 26% -> 26%
where the time goes in v3:
time: 138 us
  starting transfers between devices  48.3 us (35%)
  Pallas kernels  42.2 us (31%)
  waiting for transfers between devices  32.6 us (24%)
  blocking collectives  7.03 us (5%)
  local copies, waits for them, and re-layouts  4.35 us (3%)
  other arithmetic  2.19 us (2%)
    pallas_call x9, Pallas kernels, call(): pl.pallas_call(body, out_shape=tuple((jax.ShapeDtypeStruct(shape, dtype)...  42.2 us
    all_to_all x4, starting transfers between devices, exchange(): return lax.all_to_all(chunks, axis, 0, 0, tiled=False)  32.3 us
    all_to_all x4, waiting for transfers between devices, exchange(): return lax.all_to_all(chunks, axis, 0, 0, tiled=False)  20.5 us
    ppermute x1, waiting for transfers between devices, local(): weights_other = lax.ppermute(weights_late, ('xh', 'pipe', 'tensor'), beside)  7.39 us
    all_to_all x1, blocking collectives, exchange(): return lax.all_to_all(chunks, axis, 0, 0, tiled=False)  7.03 us
    ppermute x1, starting transfers between devices, local(): weights_other = lax.ppermute(weights_late, ('xh', 'pipe', 'tensor'), beside)  4.82 us
    ppermute x1, starting transfers between devices, local(): lax.ppermute(squares, 'pipe', SWAP)  3.96 us
    ppermute x1, starting transfers between devices, local(): up_other = lax.ppermute(up_give, ('pipe', 'tensor'), [(2, 3), (3, 2)])  3.95 us
  transfers between devices with their start and end apart: 12, of which 7 were waited for; matrix products, arithmetic and copies ran while one was open for 2% of the time, Pallas kernels for 26%

profile of v3, /device:TPU:1, one launch (start us, length us, event | category | flops | bytes accessed | tf_op | source)
XLA Modules:
  0.0 137.5 jit_solution(5654482186373592033)
XLA Ops:
  0.6 1.8 %shard_map.93 = (f32[32,256]{1,0:T(8,128)}, f32[32,256]{1,0:T(8,128)}, bf16[256,256]{1,0:T(8,128)(2,1)}) custom-call(s32[1]{0:T(128)} %bitcast.refs_0_, bf16[512,256]{1,0:T(8,128)(2,1)} %bitcast.25, f32[32,256]{1,0:T(8,128)} %bitcast.35), custom_call_target="tpu_custom_call" | custom-call | tf_op jit(solution)/shard_map/pallas_call | solution.py:118
  2.5 3.9 %collective-permute-start.1 = (bf16[256,256]{1,0:T(8,128)(2,1)}, bf16[256,256]{1,0:T(8,128)(2,1)S(1)}, u32[]{:S(2)}, u32[]{:S(2)}) collective-permute-start(bf16[256,256]{1,0:T(8,128)(2,1)} %get-tuple-element.40), channel_id=1, source_target_pairs={{2,3},{3,2},{6,7},{7,6},{10,11},{11,10},{14,15},{15,14},{18,19},{1... | collective-permute-start | bytes 393224 | tf_op jit(solution)/shard_map/ppermute | solution.py:326
  6.4 0.1 collective-permute-start
  6.5 3.0 %collective-permute-done.refs_6_ = f32[32,256]{1,0:T(8,128)S(1)} collective-permute-done((f32[32,256]{1,0:T(8,128)}, f32[32,256]{1,0:T(8,128)S(1)}, u32[]{:S(2)}, u32[]{:S(2)}) %collective-permute-start) | collective-permute-done | bytes 32800 | tf_op jit(solution)/shard_map/ppermute | solution.py:325
  9.5 0.0 copy-start.5
  9.5 0.0 collective-permute-done.1.refs_4_
  9.5 0.0 copy-start.4
  9.5 4.8 %collective-permute-start.3 = (bf16[4096,256]{1,0:T(8,128)(2,1)}, bf16[4096,256]{1,0:T(8,128)(2,1)S(1)}, u32[]{:S(2)}, u32[]{:S(2)}) collective-permute-start(bf16[4096,256]{1,0:T(8,128)(2,1)} %bitcast.29), channel_id=1, source_target_pairs={{2,7},{7,2},{3,6},{6,3},{10,15},{15,10},{11,14},{14,11},{18,23},{2... | collective-permute-start | bytes 6291464 | tf_op jit(solution)/shard_map/ppermute | solution.py:333
  14.3 0.1 collective-permute-start.2
  14.4 0.0 copy-done.5
  14.4 5.2 %shard_map.94 = (bf16[256,4096]{1,0:T(8,128)(2,1)}, f32[32,2,32,128]{3,2,1,0:T(8,128)}) custom-call(s32[1]{0:T(128)} %bitcast.refs_0_, bf16[256,4096]{1,0:T(8,128)(2,1)} %bitcast.23, f32[1,4096]{1,0:T(1,128)} %refs_2_.5, bf16[4096,256]{1,0:T(8,128)(2,1)} %bitcast.20, f32[32,256]{1,0:T(8,128)} %bitcast.36, f32[32,256]{1,0:T(8,128)} %get-tuple-element.42.refs_5_, ...), custom_call_target="tpu_custom_call" | custom-call | tf_op jit(solution)/shard_map/pallas_call | solution.py:118
  19.6 0.0 copy-done.4
  19.6 11.2 %all-to-all-start = ((f32[32,64,128]{2,1,0:T(8,128)}), f32[32,64,128]{2,1,0:T(8,128)S(1)}, u32[]{:S(2)}, u32[]{:S(2)}) async-start(f32[32,64,128]{2,1,0:T(8,128)} %bitcast.33), calls=%async_computation | async-start | bytes 2097152 | tf_op jit(solution)/shard_map/all_to_all | solution.py:46
  30.9 7.4 %collective-permute-done.3.refs_6_ = bf16[4096,256]{1,0:T(8,128)(2,1)S(1)} collective-permute-done((bf16[4096,256]{1,0:T(8,128)(2,1)}, bf16[4096,256]{1,0:T(8,128)(2,1)S(1)}, u32[]{:S(2)}, u32[]{:S(2)}) %collective-permute-start.3) | collective-permute-done | bytes 2097184 | tf_op jit(solution)/shard_map/ppermute | solution.py:333
  38.2 1.3 copy-done.3
  39.6 8.6 %shard_map.97 = bf16[256,4096]{1,0:T(8,128)(2,1)} custom-call(s32[1]{0:T(128)} %bitcast.refs_0_, bf16[256,4096]{1,0:T(8,128)(2,1)} %bitcast.24, f32[1,4096]{1,0:T(1,128)} %refs_2_.5, bf16[512,256]{1,0:T(8,128)(2,1)} %bitcast.26, bf16[256,256]{1,0:T(8,128)(2,1)} %copy-done.4, bf16[4096,256]{1,0:T(8,128)(2,1)} %bitcast.30, bf16[4096,256]{1,0:T(8,128)(2,1)} %copy-done.3), custom_call_target="tpu_custom_call" | custom-call | tf_op jit(solution)/shard_map/pallas_call | solution.py:118
  48.2 1.4 %collective-permute-start.4 = (bf16[256,4096]{1,0:T(8,128)(2,1)}, bf16[256,4096]{1,0:T(8,128)(2,1)S(1)}, u32[]{:S(2)}, u32[]{:S(2)}) collective-permute-start(bf16[256,4096]{1,0:T(8,128)(2,1)} %shard_map.97), channel_id=1, source_target_pairs={{2,0},{3,1},{6,4},{7,5},{10,8},{11,9},{14,12},{15,13},{18,16},{19,... | collective-permute-start | bytes 6291464 | tf_op jit(solution)/shard_map/ppermute | solution.py:370
  49.6 5.0 %shard_map.95.refs_4_ = bf16[4096,512]{1,0:T(8,128)(2,1)} custom-call(s32[1]{0:T(128)} %bitcast.refs_0_, bf16[256,4096]{1,0:T(8,128)(2,1)} %get-tuple-element.47.refs_1_, bf16[512,256]{1,0:T(8,128)(2,1)} %bitcast.27, bf16[4096,256]{1,0:T(8,128)(2,1)} %bitcast.21), custom_call_target="tpu_custom_call" | custom-call | tf_op jit(solution)/shard_map/pallas_call | solution.py:118
  54.6 3.3 %all-to-all-done = f32[32,64,128]{2,1,0:T(8,128)S(1)} async-done(((f32[32,64,128]{2,1,0:T(8,128)}), f32[32,64,128]{2,1,0:T(8,128)S(1)}, u32[]{:S(2)}, u32[]{:S(2)}) %all-to-all-start) | async-done | bytes 1048608 | tf_op jit(solution)/shard_map/all_to_all | solution.py:46
  57.8 1.8 %collective-permute-done.2.refs_1_ = bf16[256,4096]{1,0:T(8,128)(2,1)} collective-permute-done((bf16[256,4096]{1,0:T(8,128)(2,1)}, bf16[256,4096]{1,0:T(8,128)(2,1)}, u32[]{:S(2)}, u32[]{:S(2)}) %collective-permute-start.2) | collective-permute-done | bytes 2097184 | tf_op jit(solution)/shard_map/ppermute | solution.py:331
  59.6 0.1 reduce_sum.27
  59.7 7.0 %all_to_all.25 = f32[4,32,128]{2,1,0:T(8,128)S(1)} all-to-all(f32[4,32,128]{2,1,0:T(8,128)S(1)} %bitcast.34), channel_id=1, replica_groups=mesh['z'=8,'y'=4,'xh'=2,'pipe'=2,'tensor'=2] {'xh','tensor'}, dimensions={0} | all-to-all | bytes 131072 | tf_op jit(solution)/shard_map/all_to_all | solution.py:46
  66.8 0.9 broadcast_in_dim.36
  67.6 11.4 %all-to-all-start.2 = ((f32[32,32,128]{2,1,0:T(8,128)}), f32[32,32,128]{2,1,0:T(8,128)S(1)}, u32[]{:S(2)}, u32[]{:S(2)}) async-start(f32[32,32,128]{2,1,0:T(8,128)} %broadcast_in_dim.36), calls=%async_computation.2 | async-start | bytes 1048576 | tf_op jit(solution)/shard_map/all_to_all | solution.py:46
  79.0 6.5 %shard_map.96.refs_1_.refs_0_ = bf16[4096,512]{1,0:T(8,128)(2,1)} custom-call(s32[1]{0:T(128)} %bitcast.refs_0_, bf16[256,4096]{1,0:T(8,128)(2,1)} %collective-permute-done.2.refs_1_, f32[1,4096]{1,0:T(1,128)} %refs_2_.5, bf16[512,256]{1,0:T(8,128)(2,1)} %bitcast.28, bf16[4096,512]{1,0:T(8,128)(2,1)} %shard_map.95.refs_4_), custom_call_target="tpu_custom_call" | custom-call | tf_op jit(solution)/shard_map/pallas_call | solution.py:118
  85.5 7.5 %all-to-all-done.2.refs_0_.refs_1_ = f32[32,32,128]{2,1,0:T(8,128)S(1)} async-done(((f32[32,32,128]{2,1,0:T(8,128)}), f32[32,32,128]{2,1,0:T(8,128)S(1)}, u32[]{:S(2)}, u32[]{:S(2)}) %all-to-all-start.2) | async-done | bytes 524320 | tf_op jit(solution)/shard_map/all_to_all | solution.py:46
  93.0 0.0 collective-permute-done.4
  93.0 0.8 copy-done.2
  93.8 4.1 %shard_map.98 = (f32[8,32,256]{2,1,0:T(8,128)}, f32[32,32]{1,0:T(8,128)}) custom-call(f32[32,32,128]{2,1,0:T(8,128)} %copy-done.2, bf16[4096,512]{1,0:T(8,128)(2,1)} %shard_map.96.refs_1_.refs_0_), custom_call_target="tpu_custom_call" | custom-call | tf_op jit(solution)/shard_map/pallas_call | solution.py:118
  97.9 3.7 %all-to-all-start.3 = ((f32[8,32,256]{2,1,0:T(8,128)}), f32[8,32,256]{2,1,0:T(8,128)S(1)}, u32[]{:S(2)}, u32[]{:S(2)}) async-start(f32[8,32,256]{2,1,0:T(8,128)} %get-tuple-element.58), calls=%async_computation.3 | async-start | bytes 524288 | tf_op jit(solution)/shard_map/all_to_all | solution.py:46
  101.5 5.8 %shard_map.99 = (f32[32,4096]{1,0:T(8,128)}, bf16[4096,128]{1,0:T(8,128)(2,1)}, f32[32,32]{1,0:T(8,128)}) custom-call(f32[32,32]{1,0:T(8,128)} %get-tuple-element.59.refs_0_, f32[32,32,128]{2,1,0:T(8,128)} %copy-done.2), custom_call_target="tpu_custom_call" | custom-call | tf_op jit(solution)/shard_map/pallas_call | solution.py:118
  107.4 1.8 %all-to-all-done.3 = f32[8,32,256]{2,1,0:T(8,128)S(1)} async-done(((f32[8,32,256]{2,1,0:T(8,128)}), f32[8,32,256]{2,1,0:T(8,128)S(1)}, u32[]{:S(2)}, u32[]{:S(2)}) %all-to-all-start.3) | async-done | bytes 262176 | tf_op jit(solution)/shard_map/all_to_all | solution.py:46
  109.2 0.7 broadcast_in_dim.37
  109.9 6.0 %all-to-all-start.4 = ((f32[8,32,256]{2,1,0:T(8,128)}), f32[8,32,256]{2,1,0:T(8,128)S(1)}, u32[]{:S(2)}, u32[]{:S(2)}) async-start(f32[8,32,256]{2,1,0:T(8,128)} %broadcast_in_dim.37), calls=%async_computation.4 | async-start | bytes 524288 | tf_op jit(solution)/shard_map/all_to_all | solution.py:46
  116.0 1.5 %broadcast_select_fusion = bf16[256,4096]{1,0:T(8,128)(2,1)} fusion(bf16[256,4096]{1,0:T(8,128)(2,1)S(1)} %collective-permute-done.4, pred[]{:T(512)S(6)} %eq.3), kind=kLoop, calls=%fused_computation | loop fusion | flops 1048576 | bytes 4194305 | tf_op jit(solution)/shard_map/jit(_where)/select_n | solution.py:411
  117.4 7.9 %all-to-all-done.4.refs_0_ = f32[8,32,256]{2,1,0:T(8,128)S(1)} async-done(((f32[8,32,256]{2,1,0:T(8,128)}), f32[8,32,256]{2,1,0:T(8,128)S(1)}, u32[]{:S(2)}, u32[]{:S(2)}) %all-to-all-start.4) | async-done | bytes 262176 | tf_op jit(solution)/shard_map/all_to_all | solution.py:46
  125.3 0.0 copy-done.1
  125.4 0.5 shard_map.100
  125.9 0.0 copy-start
  125.9 0.6 copy-done
  126.5 4.0 %collective-permute-start.5 = (f32[32,256]{1,0:T(8,128)S(1)}, f32[32,256]{1,0:T(8,128)S(1)}, u32[]{:S(2)}, u32[]{:S(2)}) collective-permute-start(f32[32,256]{1,0:T(8,128)S(1)} %get-tuple-element.71), channel_id=1, source_target_pairs={{0,2},{2,0},{1,3},{3,1},{4,6},{6,4},{5,7},{7,5},{8,10},{10,8},{9,1... | collective-permute-start | bytes 98312 | tf_op jit(solution)/shard_map/ppermute | solution.py:427
  130.5 0.5 collective-permute-start.6
  131.0 1.2 collective-permute-start.7
  132.1 4.7 %shard_map.101 = bf16[4096,256]{1,0:T(8,128)(2,1)} custom-call(bf16[4096,512]{1,0:T(8,128)(2,1)} %shard_map.96.refs_1_.refs_0_, bf16[4096,128]{1,0:T(8,128)(2,1)} %get-tuple-element.72.refs_1_, bf16[128,256]{1,0:T(8,128)(2,1)} %copy-done), custom_call_target="tpu_custom_call" | custom-call | tf_op jit(solution)/shard_map/pallas_call | solution.py:118
  136.9 0.0 collective-permute-done.5
  136.9 0.0 collective-permute-done.6
  136.9 0.0 collective-permute-done.7
  136.9 0.6 multiply_bitcast_fusion
  (6 shorter events, 0.0 us)
Async XLA Ops:
  2.5 7.0 %collective-permute-start.1 = (bf16[256,256]{1,0:T(8,128)(2,1)}, bf16[256,256]{1,0:T(8,128)(2,1)S(1)}, u32[]{:S(2)}, u32[]{:S(2)}) collective-permute-start(bf16[256,256]{1,0:T(8,128)(2,1)} %get-tuple-element.40), channel_id=1, source_target_pairs={{2,3},{3,2},{6,7},{7,6},{10,11},{11,10},{14,15},{15,14},{18,19},{1... | collective-permute-start | bytes 393224 | tf_op jit(solution)/shard_map/ppermute | solution.py:326
  6.4 3.1 %collective-permute-start = (f32[32,256]{1,0:T(8,128)}, f32[32,256]{1,0:T(8,128)S(1)}, u32[]{:S(2)}, u32[]{:S(2)}) collective-permute-start(f32[32,256]{1,0:T(8,128)} %get-tuple-element.39), channel_id=1, source_target_pairs={{0,1},{1,0},{2,3},{3,2},{4,5},{5,4},{6,7},{7,6},{8,9},{9,8},{10,11... | collective-permute-start | bytes 98312 | tf_op jit(solution)/shard_map/ppermute | solution.py:325
  9.5 4.9 %copy-start.5 = (f32[32,256]{1,0:T(8,128)}, f32[32,256]{1,0:T(8,128)S(1)}, u32[]{:S(2)}) copy-start(f32[32,256]{1,0:T(8,128)S(1)} %collective-permute-done.refs_6_) | copy-start | bytes 98308
  9.5 10.1 %copy-start.4 = (bf16[256,256]{1,0:T(8,128)(2,1)}, bf16[256,256]{1,0:T(8,128)(2,1)S(1)}, u32[]{:S(2)}) copy-start(bf16[256,256]{1,0:T(8,128)(2,1)S(1)} %collective-permute-done.1.refs_4_) | copy-start | bytes 393220
  9.5 28.7 %collective-permute-start.3 = (bf16[4096,256]{1,0:T(8,128)(2,1)}, bf16[4096,256]{1,0:T(8,128)(2,1)S(1)}, u32[]{:S(2)}, u32[]{:S(2)}) collective-permute-start(bf16[4096,256]{1,0:T(8,128)(2,1)} %bitcast.29), channel_id=1, source_target_pairs={{2,7},{7,2},{3,6},{6,3},{10,15},{15,10},{11,14},{14,11},{18,23},{2... | collective-permute-start | bytes 6291464 | tf_op jit(solution)/shard_map/ppermute | solution.py:333
  14.3 45.3 %collective-permute-start.2 = (bf16[256,4096]{1,0:T(8,128)(2,1)}, bf16[256,4096]{1,0:T(8,128)(2,1)}, u32[]{:S(2)}, u32[]{:S(2)}) collective-permute-start(bf16[256,4096]{1,0:T(8,128)(2,1)} %bitcast.22), channel_id=1, source_target_pairs={{0,1},{1,0},{2,3},{3,2},{4,5},{5,4},{6,7},{7,6},{8,9},{9,8},{10,11... | collective-permute-start | bytes 6291464 | tf_op jit(solution)/shard_map/ppermute | solution.py:331
  19.6 38.2 %all-to-all-start = ((f32[32,64,128]{2,1,0:T(8,128)}), f32[32,64,128]{2,1,0:T(8,128)S(1)}, u32[]{:S(2)}, u32[]{:S(2)}) async-start(f32[32,64,128]{2,1,0:T(8,128)} %bitcast.33), calls=%async_computation | async-start | bytes 2097152 | tf_op jit(solution)/shard_map/all_to_all | solution.py:46
  38.2 1.3 copy-start.3
  48.2 44.8 %collective-permute-start.4 = (bf16[256,4096]{1,0:T(8,128)(2,1)}, bf16[256,4096]{1,0:T(8,128)(2,1)S(1)}, u32[]{:S(2)}, u32[]{:S(2)}) collective-permute-start(bf16[256,4096]{1,0:T(8,128)(2,1)} %shard_map.97), channel_id=1, source_target_pairs={{2,0},{3,1},{6,4},{7,5},{10,8},{11,9},{14,12},{15,13},{18,16},{19,... | collective-permute-start | bytes 6291464 | tf_op jit(solution)/shard_map/ppermute | solution.py:370
  67.6 25.4 %all-to-all-start.2 = ((f32[32,32,128]{2,1,0:T(8,128)}), f32[32,32,128]{2,1,0:T(8,128)S(1)}, u32[]{:S(2)}, u32[]{:S(2)}) async-start(f32[32,32,128]{2,1,0:T(8,128)} %broadcast_in_dim.36), calls=%async_computation.2 | async-start | bytes 1048576 | tf_op jit(solution)/shard_map/all_to_all | solution.py:46
  93.0 0.8 copy-start.2
  97.9 11.3 %all-to-all-start.3 = ((f32[8,32,256]{2,1,0:T(8,128)}), f32[8,32,256]{2,1,0:T(8,128)S(1)}, u32[]{:S(2)}, u32[]{:S(2)}) async-start(f32[8,32,256]{2,1,0:T(8,128)} %get-tuple-element.58), calls=%async_computation.3 | async-start | bytes 524288 | tf_op jit(solution)/shard_map/all_to_all | solution.py:46
  109.9 15.4 %all-to-all-start.4 = ((f32[8,32,256]{2,1,0:T(8,128)}), f32[8,32,256]{2,1,0:T(8,128)S(1)}, u32[]{:S(2)}, u32[]{:S(2)}) async-start(f32[8,32,256]{2,1,0:T(8,128)} %broadcast_in_dim.37), calls=%async_computation.4 | async-start | bytes 524288 | tf_op jit(solution)/shard_map/all_to_all | solution.py:46
  116.0 9.4 %copy-start.1 = (f32[32,32]{1,0:T(8,128)S(1)}, f32[32,32]{1,0:T(8,128)}, u32[]{:S(2)}) copy-start(f32[32,32]{1,0:T(8,128)} %get-tuple-element.69.refs_1_) | copy-start | bytes 12292
  125.9 0.7 copy-start
  126.5 10.4 %collective-permute-start.5 = (f32[32,256]{1,0:T(8,128)S(1)}, f32[32,256]{1,0:T(8,128)S(1)}, u32[]{:S(2)}, u32[]{:S(2)}) collective-permute-start(f32[32,256]{1,0:T(8,128)S(1)} %get-tuple-element.71), channel_id=1, source_target_pairs={{0,2},{2,0},{1,3},{3,1},{4,6},{6,4},{5,7},{7,5},{8,10},{10,8},{9,1... | collective-permute-start | bytes 98312 | tf_op jit(solution)/shard_map/ppermute | solution.py:427
  130.5 6.4 %collective-permute-start.6 = (f32[32,256]{1,0:T(8,128)S(1)}, f32[32,256]{1,0:T(8,128)S(1)}, u32[]{:S(2)}, u32[]{:S(2)}) collective-permute-start(f32[32,256]{1,0:T(8,128)S(1)} %get-tuple-element.71), channel_id=1, source_target_pairs={{0,1},{1,0},{2,3},{3,2},{4,5},{5,4},{6,7},{7,6},{8,9},{9,8},{10,11... | collective-permute-start | bytes 98312 | tf_op jit(solution)/shard_map/ppermute | solution.py:428
  131.0 5.9 %collective-permute-start.7 = (f32[32,256]{1,0:T(8,128)S(1)}, f32[32,256]{1,0:T(8,128)S(1)}, u32[]{:S(2)}, u32[]{:S(2)}) collective-permute-start(f32[32,256]{1,0:T(8,128)S(1)} %get-tuple-element.71), channel_id=1, source_target_pairs={{0,3},{3,0},{1,2},{2,1},{4,7},{7,4},{5,6},{6,5},{8,11},{11,8},{9,1... | collective-permute-start | bytes 98312 | tf_op jit(solution)/shard_map/ppermute | solution.py:429

commit v4 on v3

--- a/solution.py
+++ b/solution.py
@@ -368,11 +368,11 @@
         scalar=where,
     )
     received = lax.ppermute(section_grad, "pipe", [(1, 0)])
-    terms, activ_other, own = lax.optimization_barrier((terms, activ_other, own))
+    terms, own = lax.optimization_barrier((terms, own))
     terms = added(terms).reshape(1, n_t, rank, lanes)
     terms = jnp.broadcast_to(terms, (n_x, n_t, rank, lanes)).reshape(n_x * n_t, rank, lanes)
     summed = added(exchange(terms, ("xh", "tensor")))
-    summed, own = lax.optimization_barrier((summed, own))
+    summed, own, activ_other = lax.optimization_barrier((summed, own, activ_other))
     summed = exchange(jnp.broadcast_to(summed[None], (n_y * n_z,) + summed.shape), ("y", "z"))
     merged = call(
         merged_kernel,

time: 138 us -> 134 us (0.971)
  starting transfers between devices: 48.3 us -> 42.7 us
    all_to_all x4, starting transfers between devices: 32.3 us -> 28 us  [exchange(): return lax.all_to_all(chunks, axis, 0, 0, tiled=False)]
    all_to_all x4, waiting for transfers between devices: 20.5 us -> 23.2 us  [exchange(): return lax.all_to_all(chunks, axis, 0, 0, tiled=False)]
    ppermute x1, waiting for transfers between devices: 1.79 us -> 0.01 us  [local(): activ_other = lax.ppermute(activ_late, 'tensor', SWAP)]
  transfers between devices with their start and end apart: 12 -> 12, of which waited for: 7 -> 6; matrix products, arithmetic and copies ran while one was open for 2% -> 2% of each run, Pallas kernels for 26% -> 27%
where the time goes in v4:
time: 134 us
  starting transfers between devices  42.7 us (32%)
  Pallas kernels  42.3 us (32%)
  waiting for transfers between devices  33.6 us (25%)
  blocking collectives  7.77 us (6%)
  local copies, waits for them, and re-layouts  4.35 us (3%)
  other arithmetic  2.19 us (2%)
    pallas_call x9, Pallas kernels, call(): pl.pallas_call(body, out_shape=tuple((jax.ShapeDtypeStruct(shape, dtype)...  42.3 us
    all_to_all x4, starting transfers between devices, exchange(): return lax.all_to_all(chunks, axis, 0, 0, tiled=False)  28 us
    all_to_all x4, waiting for transfers between devices, exchange(): return lax.all_to_all(chunks, axis, 0, 0, tiled=False)  23.2 us
    all_to_all x1, blocking collectives, exchange(): return lax.all_to_all(chunks, axis, 0, 0, tiled=False)  7.77 us
    ppermute x1, waiting for transfers between devices, local(): weights_other = lax.ppermute(weights_late, ('xh', 'pipe', 'tensor'), beside)  7.39 us
    ppermute x1, starting transfers between devices, local(): weights_other = lax.ppermute(weights_late, ('xh', 'pipe', 'tensor'), beside)  4.82 us
    ppermute x1, starting transfers between devices, local(): up_other = lax.ppermute(up_give, ('pipe', 'tensor'), [(2, 3), (3, 2)])  3.95 us
    ppermute x1, waiting for transfers between devices, local(): other_v = lax.ppermute(give_v, 'tensor', SWAP)  2.96 us
  transfers between devices with their start and end apart: 12, of which 6 were waited for; matrix products, arithmetic and copies ran while one was open for 2% of the time, Pallas kernels for 27%

profile of v4, /device:TPU:1, one launch (start us, length us, event | category | flops | bytes accessed | tf_op | source)
XLA Modules:
  0.0 133.6 jit_solution(13914539348346339716)
XLA Ops:
  0.6 1.8 %shard_map.93 = (f32[32,256]{1,0:T(8,128)}, f32[32,256]{1,0:T(8,128)}, bf16[256,256]{1,0:T(8,128)(2,1)}) custom-call(s32[1]{0:T(128)} %bitcast.refs_0_, bf16[512,256]{1,0:T(8,128)(2,1)} %bitcast.25, f32[32,256]{1,0:T(8,128)} %bitcast.35), custom_call_target="tpu_custom_call" | custom-call | tf_op jit(solution)/shard_map/pallas_call | solution.py:118
  2.5 3.9 %collective-permute-start.1 = (bf16[256,256]{1,0:T(8,128)(2,1)}, bf16[256,256]{1,0:T(8,128)(2,1)S(1)}, u32[]{:S(2)}, u32[]{:S(2)}) collective-permute-start(bf16[256,256]{1,0:T(8,128)(2,1)} %get-tuple-element.40), channel_id=1, source_target_pairs={{2,3},{3,2},{6,7},{7,6},{10,11},{11,10},{14,15},{15,14},{18,19},{1... | collective-permute-start | bytes 393224 | tf_op jit(solution)/shard_map/ppermute | solution.py:326
  6.4 0.1 collective-permute-start
  6.5 3.0 %collective-permute-done.refs_6_ = f32[32,256]{1,0:T(8,128)S(1)} collective-permute-done((f32[32,256]{1,0:T(8,128)}, f32[32,256]{1,0:T(8,128)S(1)}, u32[]{:S(2)}, u32[]{:S(2)}) %collective-permute-start) | collective-permute-done | bytes 32800 | tf_op jit(solution)/shard_map/ppermute | solution.py:325
  9.5 0.0 copy-start.5
  9.5 0.0 collective-permute-done.1.refs_4_
  9.5 0.0 copy-start.4
  9.5 4.8 %collective-permute-start.3 = (bf16[4096,256]{1,0:T(8,128)(2,1)}, bf16[4096,256]{1,0:T(8,128)(2,1)S(1)}, u32[]{:S(2)}, u32[]{:S(2)}) collective-permute-start(bf16[4096,256]{1,0:T(8,128)(2,1)} %bitcast.29), channel_id=1, source_target_pairs={{2,7},{7,2},{3,6},{6,3},{10,15},{15,10},{11,14},{14,11},{18,23},{2... | collective-permute-start | bytes 6291464 | tf_op jit(solution)/shard_map/ppermute | solution.py:333
  14.3 0.1 collective-permute-start.2
  14.4 0.0 copy-done.5
  14.4 5.2 %shard_map.94 = (bf16[256,4096]{1,0:T(8,128)(2,1)}, f32[32,2,32,128]{3,2,1,0:T(8,128)}) custom-call(s32[1]{0:T(128)} %bitcast.refs_0_, bf16[256,4096]{1,0:T(8,128)(2,1)} %bitcast.23, f32[1,4096]{1,0:T(1,128)} %refs_2_.5, bf16[4096,256]{1,0:T(8,128)(2,1)} %bitcast.20, f32[32,256]{1,0:T(8,128)} %bitcast.36, f32[32,256]{1,0:T(8,128)} %get-tuple-element.42.refs_5_, ...), custom_call_target="tpu_custom_call" | custom-call | tf_op jit(solution)/shard_map/pallas_call | solution.py:118
  19.6 0.0 copy-done.4
  19.6 11.2 %all-to-all-start = ((f32[32,64,128]{2,1,0:T(8,128)}), f32[32,64,128]{2,1,0:T(8,128)S(1)}, u32[]{:S(2)}, u32[]{:S(2)}) async-start(f32[32,64,128]{2,1,0:T(8,128)} %bitcast.33), calls=%async_computation | async-start | bytes 2097152 | tf_op jit(solution)/shard_map/all_to_all | solution.py:46
  30.9 7.4 %collective-permute-done.3.refs_6_ = bf16[4096,256]{1,0:T(8,128)(2,1)S(1)} collective-permute-done((bf16[4096,256]{1,0:T(8,128)(2,1)}, bf16[4096,256]{1,0:T(8,128)(2,1)S(1)}, u32[]{:S(2)}, u32[]{:S(2)}) %collective-permute-start.3) | collective-permute-done | bytes 2097184 | tf_op jit(solution)/shard_map/ppermute | solution.py:333
  38.2 1.3 copy-done.3
  39.6 8.6 %shard_map.97 = bf16[256,4096]{1,0:T(8,128)(2,1)} custom-call(s32[1]{0:T(128)} %bitcast.refs_0_, bf16[256,4096]{1,0:T(8,128)(2,1)} %bitcast.24, f32[1,4096]{1,0:T(1,128)} %refs_2_.5, bf16[512,256]{1,0:T(8,128)(2,1)} %bitcast.26, bf16[256,256]{1,0:T(8,128)(2,1)} %copy-done.4, bf16[4096,256]{1,0:T(8,128)(2,1)} %bitcast.30, bf16[4096,256]{1,0:T(8,128)(2,1)} %copy-done.3), custom_call_target="tpu_custom_call" | custom-call | tf_op jit(solution)/shard_map/pallas_call | solution.py:118
  48.2 1.4 %collective-permute-start.4 = (bf16[256,4096]{1,0:T(8,128)(2,1)}, bf16[256,4096]{1,0:T(8,128)(2,1)S(1)}, u32[]{:S(2)}, u32[]{:S(2)}) collective-permute-start(bf16[256,4096]{1,0:T(8,128)(2,1)} %shard_map.97), channel_id=1, source_target_pairs={{2,0},{3,1},{6,4},{7,5},{10,8},{11,9},{14,12},{15,13},{18,16},{19,... | collective-permute-start | bytes 6291464 | tf_op jit(solution)/shard_map/ppermute | solution.py:370
  49.6 5.0 %shard_map.95.refs_4_ = bf16[4096,512]{1,0:T(8,128)(2,1)} custom-call(s32[1]{0:T(128)} %bitcast.refs_0_, bf16[256,4096]{1,0:T(8,128)(2,1)} %get-tuple-element.47.refs_1_, bf16[512,256]{1,0:T(8,128)(2,1)} %bitcast.27, bf16[4096,256]{1,0:T(8,128)(2,1)} %bitcast.21), custom_call_target="tpu_custom_call" | custom-call | tf_op jit(solution)/shard_map/pallas_call | solution.py:118
  54.6 3.3 %all-to-all-done = f32[32,64,128]{2,1,0:T(8,128)S(1)} async-done(((f32[32,64,128]{2,1,0:T(8,128)}), f32[32,64,128]{2,1,0:T(8,128)S(1)}, u32[]{:S(2)}, u32[]{:S(2)}) %all-to-all-start) | async-done | bytes 1048608 | tf_op jit(solution)/shard_map/all_to_all | solution.py:46
  57.8 0.1 reduce_sum.27
  57.9 7.8 %all_to_all.25 = f32[4,32,128]{2,1,0:T(8,128)S(1)} all-to-all(f32[4,32,128]{2,1,0:T(8,128)S(1)} %bitcast.34), channel_id=1, replica_groups=mesh['z'=8,'y'=4,'xh'=2,'pipe'=2,'tensor'=2] {'xh','tensor'}, dimensions={0} | all-to-all | bytes 131072 | tf_op jit(solution)/shard_map/all_to_all | solution.py:46
  65.7 0.0 collective-permute-done.2.refs_1_
  65.7 0.9 broadcast_in_dim.36
  66.6 8.6 %all-to-all-start.2 = ((f32[32,32,128]{2,1,0:T(8,128)}), f32[32,32,128]{2,1,0:T(8,128)S(1)}, u32[]{:S(2)}, u32[]{:S(2)}) async-start(f32[32,32,128]{2,1,0:T(8,128)} %broadcast_in_dim.36), calls=%async_computation.2 | async-start | bytes 1048576 | tf_op jit(solution)/shard_map/all_to_all | solution.py:46
  75.1 6.5 %shard_map.96.refs_1_.refs_0_ = bf16[4096,512]{1,0:T(8,128)(2,1)} custom-call(s32[1]{0:T(128)} %bitcast.refs_0_, bf16[256,4096]{1,0:T(8,128)(2,1)} %collective-permute-done.2.refs_1_, f32[1,4096]{1,0:T(1,128)} %refs_2_.5, bf16[512,256]{1,0:T(8,128)(2,1)} %bitcast.28, bf16[4096,512]{1,0:T(8,128)(2,1)} %shard_map.95.refs_4_), custom_call_target="tpu_custom_call" | custom-call | tf_op jit(solution)/shard_map/pallas_call | solution.py:118
  81.7 9.3 %all-to-all-done.2.refs_0_.refs_1_ = f32[32,32,128]{2,1,0:T(8,128)S(1)} async-done(((f32[32,32,128]{2,1,0:T(8,128)}), f32[32,32,128]{2,1,0:T(8,128)S(1)}, u32[]{:S(2)}, u32[]{:S(2)}) %all-to-all-start.2) | async-done | bytes 524320 | tf_op jit(solution)/shard_map/all_to_all | solution.py:46
  91.0 0.0 collective-permute-done.4
  91.0 0.8 copy-done.2
  91.8 4.1 %shard_map.98 = (f32[8,32,256]{2,1,0:T(8,128)}, f32[32,32]{1,0:T(8,128)}) custom-call(f32[32,32,128]{2,1,0:T(8,128)} %copy-done.2, bf16[4096,512]{1,0:T(8,128)(2,1)} %shard_map.96.refs_1_.refs_0_), custom_call_target="tpu_custom_call" | custom-call | tf_op jit(solution)/shard_map/pallas_call | solution.py:118
  95.9 3.4 %all-to-all-start.3 = ((f32[8,32,256]{2,1,0:T(8,128)}), f32[8,32,256]{2,1,0:T(8,128)S(1)}, u32[]{:S(2)}, u32[]{:S(2)}) async-start(f32[8,32,256]{2,1,0:T(8,128)} %get-tuple-element.58), calls=%async_computation.3 | async-start | bytes 524288 | tf_op jit(solution)/shard_map/all_to_all | solution.py:46
  99.3 5.8 %shard_map.99 = (f32[32,4096]{1,0:T(8,128)}, bf16[4096,128]{1,0:T(8,128)(2,1)}, f32[32,32]{1,0:T(8,128)}) custom-call(f32[32,32]{1,0:T(8,128)} %get-tuple-element.59.refs_0_, f32[32,32,128]{2,1,0:T(8,128)} %copy-done.2), custom_call_target="tpu_custom_call" | custom-call | tf_op jit(solution)/shard_map/pallas_call | solution.py:118
  105.1 1.9 %all-to-all-done.3 = f32[8,32,256]{2,1,0:T(8,128)S(1)} async-done(((f32[8,32,256]{2,1,0:T(8,128)}), f32[8,32,256]{2,1,0:T(8,128)S(1)}, u32[]{:S(2)}, u32[]{:S(2)}) %all-to-all-start.3) | async-done | bytes 262176 | tf_op jit(solution)/shard_map/all_to_all | solution.py:46
  107.0 0.7 broadcast_in_dim.37
  107.8 4.8 %all-to-all-start.4 = ((f32[8,32,256]{2,1,0:T(8,128)}), f32[8,32,256]{2,1,0:T(8,128)S(1)}, u32[]{:S(2)}, u32[]{:S(2)}) async-start(f32[8,32,256]{2,1,0:T(8,128)} %broadcast_in_dim.37), calls=%async_computation.4 | async-start | bytes 524288 | tf_op jit(solution)/shard_map/all_to_all | solution.py:46
  112.6 1.5 %broadcast_select_fusion = bf16[256,4096]{1,0:T(8,128)(2,1)} fusion(bf16[256,4096]{1,0:T(8,128)(2,1)S(1)} %collective-permute-done.4, pred[]{:T(512)S(6)} %eq.3), kind=kLoop, calls=%fused_computation | loop fusion | flops 1048576 | bytes 4194305 | tf_op jit(solution)/shard_map/jit(_where)/select_n | solution.py:411
  114.0 8.7 %all-to-all-done.4.refs_0_ = f32[8,32,256]{2,1,0:T(8,128)S(1)} async-done(((f32[8,32,256]{2,1,0:T(8,128)}), f32[8,32,256]{2,1,0:T(8,128)S(1)}, u32[]{:S(2)}, u32[]{:S(2)}) %all-to-all-start.4) | async-done | bytes 262176 | tf_op jit(solution)/shard_map/all_to_all | solution.py:46
  122.8 0.0 copy-done.1
  122.8 0.5 shard_map.100
  123.3 0.0 copy-start
  123.3 0.6 copy-done
  123.9 2.6 %collective-permute-start.5 = (f32[32,256]{1,0:T(8,128)S(1)}, f32[32,256]{1,0:T(8,128)S(1)}, u32[]{:S(2)}, u32[]{:S(2)}) collective-permute-start(f32[32,256]{1,0:T(8,128)S(1)} %get-tuple-element.71), channel_id=1, source_target_pairs={{0,2},{2,0},{1,3},{3,1},{4,6},{6,4},{5,7},{7,5},{8,10},{10,8},{9,1... | collective-permute-start | bytes 98312 | tf_op jit(solution)/shard_map/ppermute | solution.py:427
  126.6 0.3 collective-permute-start.6
  126.9 1.3 collective-permute-start.7
  128.2 4.8 %shard_map.101 = bf16[4096,256]{1,0:T(8,128)(2,1)} custom-call(bf16[4096,512]{1,0:T(8,128)(2,1)} %shard_map.96.refs_1_.refs_0_, bf16[4096,128]{1,0:T(8,128)(2,1)} %get-tuple-element.72.refs_1_, bf16[128,256]{1,0:T(8,128)(2,1)} %copy-done), custom_call_target="tpu_custom_call" | custom-call | tf_op jit(solution)/shard_map/pallas_call | solution.py:118
  133.0 0.0 collective-permute-done.5
  133.0 0.0 collective-permute-done.6
  133.0 0.0 collective-permute-done.7
  133.0 0.6 multiply_bitcast_fusion
  (6 shorter events, 0.0 us)
Async XLA Ops:
  2.5 7.0 %collective-permute-start.1 = (bf16[256,256]{1,0:T(8,128)(2,1)}, bf16[256,256]{1,0:T(8,128)(2,1)S(1)}, u32[]{:S(2)}, u32[]{:S(2)}) collective-permute-start(bf16[256,256]{1,0:T(8,128)(2,1)} %get-tuple-element.40), channel_id=1, source_target_pairs={{2,3},{3,2},{6,7},{7,6},{10,11},{11,10},{14,15},{15,14},{18,19},{1... | collective-permute-start | bytes 393224 | tf_op jit(solution)/shard_map/ppermute | solution.py:326
  6.4 3.1 %collective-permute-start = (f32[32,256]{1,0:T(8,128)}, f32[32,256]{1,0:T(8,128)S(1)}, u32[]{:S(2)}, u32[]{:S(2)}) collective-permute-start(f32[32,256]{1,0:T(8,128)} %get-tuple-element.39), channel_id=1, source_target_pairs={{0,1},{1,0},{2,3},{3,2},{4,5},{5,4},{6,7},{7,6},{8,9},{9,8},{10,11... | collective-permute-start | bytes 98312 | tf_op jit(solution)/shard_map/ppermute | solution.py:325
  9.5 4.9 %copy-start.5 = (f32[32,256]{1,0:T(8,128)}, f32[32,256]{1,0:T(8,128)S(1)}, u32[]{:S(2)}) copy-start(f32[32,256]{1,0:T(8,128)S(1)} %collective-permute-done.refs_6_) | copy-start | bytes 98308
  9.5 10.1 %copy-start.4 = (bf16[256,256]{1,0:T(8,128)(2,1)}, bf16[256,256]{1,0:T(8,128)(2,1)S(1)}, u32[]{:S(2)}) copy-start(bf16[256,256]{1,0:T(8,128)(2,1)S(1)} %collective-permute-done.1.refs_4_) | copy-start | bytes 393220
  9.5 28.7 %collective-permute-start.3 = (bf16[4096,256]{1,0:T(8,128)(2,1)}, bf16[4096,256]{1,0:T(8,128)(2,1)S(1)}, u32[]{:S(2)}, u32[]{:S(2)}) collective-permute-start(bf16[4096,256]{1,0:T(8,128)(2,1)} %bitcast.29), channel_id=1, source_target_pairs={{2,7},{7,2},{3,6},{6,3},{10,15},{15,10},{11,14},{14,11},{18,23},{2... | collective-permute-start | bytes 6291464 | tf_op jit(solution)/shard_map/ppermute | solution.py:333
  14.3 51.4 %collective-permute-start.2 = (bf16[256,4096]{1,0:T(8,128)(2,1)}, bf16[256,4096]{1,0:T(8,128)(2,1)}, u32[]{:S(2)}, u32[]{:S(2)}) collective-permute-start(bf16[256,4096]{1,0:T(8,128)(2,1)} %bitcast.22), channel_id=1, source_target_pairs={{0,1},{1,0},{2,3},{3,2},{4,5},{5,4},{6,7},{7,6},{8,9},{9,8},{10,11... | collective-permute-start | bytes 6291464 | tf_op jit(solution)/shard_map/ppermute | solution.py:331
  19.6 38.2 %all-to-all-start = ((f32[32,64,128]{2,1,0:T(8,128)}), f32[32,64,128]{2,1,0:T(8,128)S(1)}, u32[]{:S(2)}, u32[]{:S(2)}) async-start(f32[32,64,128]{2,1,0:T(8,128)} %bitcast.33), calls=%async_computation | async-start | bytes 2097152 | tf_op jit(solution)/shard_map/all_to_all | solution.py:46
  38.2 1.3 copy-start.3
  48.2 42.8 %collective-permute-start.4 = (bf16[256,4096]{1,0:T(8,128)(2,1)}, bf16[256,4096]{1,0:T(8,128)(2,1)S(1)}, u32[]{:S(2)}, u32[]{:S(2)}) collective-permute-start(bf16[256,4096]{1,0:T(8,128)(2,1)} %shard_map.97), channel_id=1, source_target_pairs={{2,0},{3,1},{6,4},{7,5},{10,8},{11,9},{14,12},{15,13},{18,16},{19,... | collective-permute-start | bytes 6291464 | tf_op jit(solution)/shard_map/ppermute | solution.py:370
  66.6 24.4 %all-to-all-start.2 = ((f32[32,32,128]{2,1,0:T(8,128)}), f32[32,32,128]{2,1,0:T(8,128)S(1)}, u32[]{:S(2)}, u32[]{:S(2)}) async-start(f32[32,32,128]{2,1,0:T(8,128)} %broadcast_in_dim.36), calls=%async_computation.2 | async-start | bytes 1048576 | tf_op jit(solution)/shard_map/all_to_all | solution.py:46
  91.0 0.8 copy-start.2
  95.9 11.2 %all-to-all-start.3 = ((f32[8,32,256]{2,1,0:T(8,128)}), f32[8,32,256]{2,1,0:T(8,128)S(1)}, u32[]{:S(2)}, u32[]{:S(2)}) async-start(f32[8,32,256]{2,1,0:T(8,128)} %get-tuple-element.58), calls=%async_computation.3 | async-start | bytes 524288 | tf_op jit(solution)/shard_map/all_to_all | solution.py:46
  107.8 15.0 %all-to-all-start.4 = ((f32[8,32,256]{2,1,0:T(8,128)}), f32[8,32,256]{2,1,0:T(8,128)S(1)}, u32[]{:S(2)}, u32[]{:S(2)}) async-start(f32[8,32,256]{2,1,0:T(8,128)} %broadcast_in_dim.37), calls=%async_computation.4 | async-start | bytes 524288 | tf_op jit(solution)/shard_map/all_to_all | solution.py:46
  112.6 10.2 %copy-start.1 = (f32[32,32]{1,0:T(8,128)S(1)}, f32[32,32]{1,0:T(8,128)}, u32[]{:S(2)}) copy-start(f32[32,32]{1,0:T(8,128)} %get-tuple-element.69.refs_1_) | copy-start | bytes 12292
  123.3 0.7 copy-start
  123.9 9.1 %collective-permute-start.5 = (f32[32,256]{1,0:T(8,128)S(1)}, f32[32,256]{1,0:T(8,128)S(1)}, u32[]{:S(2)}, u32[]{:S(2)}) collective-permute-start(f32[32,256]{1,0:T(8,128)S(1)} %get-tuple-element.71), channel_id=1, source_target_pairs={{0,2},{2,0},{1,3},{3,1},{4,6},{6,4},{5,7},{7,5},{8,10},{10,8},{9,1... | collective-permute-start | bytes 98312 | tf_op jit(solution)/shard_map/ppermute | solution.py:427
  126.6 6.4 %collective-permute-start.6 = (f32[32,256]{1,0:T(8,128)S(1)}, f32[32,256]{1,0:T(8,128)S(1)}, u32[]{:S(2)}, u32[]{:S(2)}) collective-permute-start(f32[32,256]{1,0:T(8,128)S(1)} %get-tuple-element.71), channel_id=1, source_target_pairs={{0,1},{1,0},{2,3},{3,2},{4,5},{5,4},{6,7},{7,6},{8,9},{9,8},{10,11... | collective-permute-start | bytes 98312 | tf_op jit(solution)/shard_map/ppermute | solution.py:428
  126.9 6.1 %collective-permute-start.7 = (f32[32,256]{1,0:T(8,128)S(1)}, f32[32,256]{1,0:T(8,128)S(1)}, u32[]{:S(2)}, u32[]{:S(2)}) collective-permute-start(f32[32,256]{1,0:T(8,128)S(1)} %get-tuple-element.71), channel_id=1, source_target_pairs={{0,3},{3,0},{1,2},{2,1},{4,7},{7,4},{5,6},{6,5},{8,11},{11,8},{9,1... | collective-permute-start | bytes 98312 | tf_op jit(solution)/shard_map/ppermute | solution.py:429
